TPU v7x, 32 devices: a whole 2x2x4 slice. The times are simulated.
32 devices in a mesh: head: 4 (over z), sq: 8 (over y, x, core).
Axes of the slice: x: 2, y: 2, z: 4, core: 2. Of those that a mesh axis runs over, the one named last changes fastest.
Arguments:
- layer_in: bfloat16 [8192, 2048], P(('sq', 'head')), may hold values from -6 to 6
- norm1_gain: bfloat16 [2048], P('sq'), may hold values from 0.5 to 1.5
- norm1_bias: bfloat16 [2048], P('sq'), may hold values from -1.1953125 to 1.1953125
- w_query: bfloat16 [2048, 2048], P('sq', 'head'), may hold values from -0.125 to 0.125
- w_key: bfloat16 [2048, 2048], P('sq', 'head'), may hold values from -0.125 to 0.125
- w_value: bfloat16 [2048, 4096], P('sq', 'head'), may hold values from -0.125 to 0.125
- w_swish: bfloat16 [2048, 4096], P('sq', 'head'), may hold values from -0.125 to 0.125
- w_out: bfloat16 [4096, 2048], P('head', 'sq'), may hold values from -0.1875 to 0.1875
- norm2_gain: bfloat16 [2048], P('sq'), may hold values from 0.5 to 1.5
- norm2_bias: bfloat16 [2048], P('sq'), may hold values from -1.1953125 to 1.1953125
- w_gate: bfloat16 [2048, 4096], P('sq', 'head'), may hold values from -0.125 to 0.125
- w_up: bfloat16 [2048, 4096], P('sq', 'head'), may hold values from -0.125 to 0.125
- w_down: bfloat16 [4096, 2048], P('head', 'sq'), may hold values from -0.1875 to 0.1875
- cotangent: bfloat16 [8192, 2048], P(('sq', 'head')), may hold values from -6 to 6
Outputs:
- result: bfloat16 [8192, 2048], P(('sq', 'head'))
- grad_in: float32 [8192, 2048], P(('sq', 'head'))
- grad_norm1_gain: float32 [2048], P(('head', 'sq'))
- grad_norm1_bias: float32 [2048], P(('head', 'sq'))
- grad_query: float32 [2048, 2048], P('sq', 'head')
- grad_key: float32 [2048, 2048], P('sq', 'head')
- grad_value: float32 [2048, 4096], P('sq', 'head')
- grad_swish: float32 [2048, 4096], P('sq', 'head')
- grad_out: float32 [4096, 2048], P('head', 'sq')
- grad_norm2_gain: float32 [2048], P('sq')
- grad_norm2_bias: float32 [2048], P('sq')
- grad_gate: float32 [2048, 4096], P('sq', 'head')
- grad_up: float32 [2048, 4096], P('sq', 'head')
- grad_down: float32 [4096, 2048], P('head', 'sq')
All inputs are finite; a program needn't handle non-finite values.
Results may differ from a plain program's by a relative error of at most 0.025.
Values may be sent and summed in bfloat16 or wider, within the bound.
No kernel may reach another device: no remote copies, remote signals or barrier semaphores. Data moves between devices by JAX's collectives and lax.ppermute only.
A program may use at most 320 MiB of HBM per device.

v0:
```python
import functools

import jax
import jax.numpy as jnp
from jax import lax
from jax.experimental import pallas as pl
from jax.experimental.pallas import tpu as pltpu
from jax.sharding import PartitionSpec as P

KD = 256
VD = 512
CHUNK = 256


eps_layer = 1e-05
eps_group = 1e-06
low = jnp.bfloat16
wide = jnp.float32


def mask_of(slot, count):
    bits = count.bit_length() - 1
    return ((slot << 1) & (count - 1)) | (slot >> (bits - 1))


def slot_of(mask, count):
    bits = count.bit_length() - 1
    return (mask >> 1) | ((mask & 1) << (bits - 1))


def flip(value, mask):
    count = lax.axis_size("sq")
    return lax.ppermute(value, "sq", [(i, i ^ mask) for i in range(count)])


def route(swapped):
    count = lax.axis_size("sq")
    lower = list(range(count.bit_length() - 2))
    return lower[::-1] if swapped else lower


def own_order(values):
    count = lax.axis_size("sq")
    width = values.shape[-1] // count
    place = lax.axis_index("sq")
    return jnp.concatenate(
        [
            lax.dynamic_slice_in_dim(values, (place ^ mask_of(s, count)) * width, width, -1)
            for s in range(count)
        ],
        axis=-1,
    )


def true_order(values):
    count = lax.axis_size("sq")
    width = values.shape[-1] // count
    place = lax.axis_index("sq")
    return jnp.concatenate(
        [
            lax.dynamic_slice_in_dim(values, slot_of(place ^ b, count) * width, width, -1)
            for b in range(count)
        ],
        axis=-1,
    )


class Box:
    def __init__(self, value):
        self.value = value

    def get(self):
        return [self.value]

    def put(self, values):
        (self.value,) = values


class Many:
    def __init__(self, *values):
        self.value = list(values)

    def get(self):
        return self.value

    def put(self, values):
        self.value = list(values)


class Gather:
    def __init__(self, *shards):
        self.count = lax.axis_size("sq")
        self.top = self.count // 2
        self.pieces = [{0: shard} for shard in shards]
        self.far = []
        self.todo = []
        for swapped in (False, True):
            slots, units = [0], []
            for bit in route(swapped):
                units += [(s, bit) for s in slots]
                slots += [s | 1 << bit for s in slots]
            self.todo.append(units)

    def send(self, times=1):
        for k, held in enumerate(self.pieces):
            for slot, bit in self.todo[k][:times]:
                held[slot | 1 << bit] = flip(held[slot], mask_of(1 << bit, self.count))
            self.todo[k] = self.todo[k][times:]

    def rest(self):
        self.send(len(self.todo[0]))

    def core(self):
        sent = [s for slots, _ in self.far for s in slots]
        ready = [s for s in range(self.top) if s not in sent and all(s in h for h in self.pieces)]
        if ready:
            both = stack([held[s] for s in ready for held in self.pieces])
            self.far.append((ready, flip(both, mask_of(self.top, self.count))))

    def refs(self):
        operands = [held[s] for held in self.pieces for s in range(self.top)]
        places = [[(k * self.top + s, None) for s in range(self.top)] for k in range(2)]
        for k in range(2):
            for s in range(self.top):
                for g, (slots, _) in enumerate(self.far):
                    if s in slots:
                        places[k].append((2 * self.top + g, 2 * slots.index(s) + k))
        return operands + [array for _, array in self.far], places

    def get(self):
        near = [held[s] for held in self.pieces for s in sorted(held)]
        return near + [array for _, array in self.far]

    def put(self, values):
        values = iter(values)
        self.pieces = [{s: next(values) for s in sorted(held)} for held in self.pieces]
        self.far = [(slots, next(values)) for slots, _ in self.far]


class Small:
    def __init__(self, shard):
        self.count = lax.axis_size("sq")
        self.pieces = {0: shard}
        bits = self.count.bit_length() - 1
        self.todo = [bits - 1, *range(bits - 1)]

    def send(self):
        if self.todo:
            bit, self.todo = self.todo[0], self.todo[1:]
            slots = sorted(self.pieces)
            far = flip(jnp.stack([self.pieces[s] for s in slots]), mask_of(1 << bit, self.count))
            for k, s in enumerate(slots):
                self.pieces[s | 1 << bit] = far[k]

    def rest(self):
        while self.todo:
            self.send()

    def get(self):
        return [self.pieces[s] for s in sorted(self.pieces)]

    def put(self, values):
        self.pieces = dict(zip(sorted(self.pieces), values))


class Scatter:
    def __init__(self, lefts, rights):
        self.count = lax.axis_size("sq")
        top = self.count // 2
        self.rows = lefts[0].shape[1] // self.count
        self.todo = [route(k == 1)[::-1] for k in range(2)]
        self.slots = [list(range(top)) for _ in range(2)]
        self.arrived = False
        self.sources = lefts, rights
        self.held = [outer_half(lefts, rights, 1)]

    def core(self):
        self.held = [flip(self.held[0], mask_of(self.count // 2, self.count))]

    def near(self):
        self.held = outer_half(*self.sources, 0, self.held[0], self.rows, self.part())

    def part(self):
        return [[s >> self.todo[k][0] & 1 for s in self.slots[k]] for k in range(2)]

    def send(self, lazy=False):
        self.merge()
        for k in range(2):
            bit, self.todo[k] = self.todo[k][0], self.todo[k][1:]
            self.held[2 * k + 1] = flip(self.held[2 * k + 1], mask_of(1 << bit, self.count))
            self.slots[k] = [s for s in self.slots[k] if not s >> bit & 1]
        self.arrived = True
        if not lazy:
            self.merge()

    def merge(self):
        if self.arrived:
            bits = self.part() if self.todo[0] else None
            self.held = list(split(self.held[::2], self.held[1::2], self.rows, bits))
            self.arrived = False

    def rest(self):
        self.merge()
        while self.todo[0]:
            self.send()
        return self.held

    def get(self):
        return list(self.held)

    def put(self, values):
        self.held = list(values)


def settle(*things):
    values = lax.optimization_barrier(tuple(v for t in things for v in t.get()))
    values = list(values)
    for thing in things:
        size = len(thing.get())
        thing.put(values[:size])
        values = values[size:]


def ring_step(value):
    count = lax.axis_size("head")
    return lax.ppermute(value, "head", [(i, (i + 1) % count) for i in range(count)])


def sum_others(values, axis, masks):
    count = lax.axis_size(axis)
    held = [values]
    held += [lax.ppermute(values, axis, [(i, i ^ m) for i in range(count)]) for m in masks]
    while len(held) > 1:
        held = [a + b for a, b in zip(held[::2], held[1::2])]
    return held[0]


def layer_norm(values, weight_gain, weight_shift):
    centered = values - jnp.mean(values, axis=-1, keepdims=True)
    spread = lax.rsqrt(jnp.mean(centered * centered, axis=-1, keepdims=True) + eps_layer)
    return centered * spread * weight_gain + weight_shift


def gelu_gate(pre_gate, pre_up):
    return jax.nn.gelu(pre_gate) * pre_up


def log_decay(first_head, head_count):
    head_ids = (first_head + jnp.arange(head_count)).astype(jnp.float32)
    return jnp.log(1.0 - jnp.exp2(-5.0 - head_ids))


def project(left_side, right_side):
    return jnp.dot(left_side, right_side, preferred_element_type=jnp.float32)


def outer_sum(left_side, right_side):
    return lax.dot_general(
        left_side, right_side, (((0,), (0,)), ((), ())), preferred_element_type=jnp.float32
    )


def back_project(gradient, weight):
    return lax.dot_general(
        gradient, weight, (((1,), (1,)), ((), ())), preferred_element_type=jnp.float32
    )


def swap_head(value, mask):
    count = lax.axis_size("head")
    return lax.ppermute(value, "head", [(i, i ^ mask) for i in range(count)])


def stack_kernel(*refs):
    for k, ref in enumerate(refs[:-1]):
        refs[-1][k] = ref[...]


def stack(pieces):
    vmem = pl.BlockSpec(memory_space=pltpu.VMEM)
    return pl.pallas_call(
        stack_kernel,
        in_specs=[vmem] * len(pieces),
        out_specs=vmem,
        out_shape=jax.ShapeDtypeStruct((len(pieces),) + pieces[0].shape, pieces[0].dtype),
        compiler_params=pltpu.CompilerParams(vmem_limit_bytes=16 * 2**20),
        cost_estimate=brief,
    )(*pieces)


def beside_kernel(*refs):
    begin = 0
    for ref in refs[:-1]:
        refs[-1][:, pl.ds(begin, ref.shape[1])] = ref[...]
        begin += ref.shape[1]


def beside(pieces):
    vmem = pl.BlockSpec(memory_space=pltpu.VMEM)
    columns = sum(p.shape[1] for p in pieces)
    return pl.pallas_call(
        beside_kernel,
        in_specs=[vmem] * len(pieces),
        out_specs=vmem,
        out_shape=jax.ShapeDtypeStruct((pieces[0].shape[0], columns), pieces[0].dtype),
        compiler_params=pltpu.CompilerParams(vmem_limit_bytes=16 * 2**20),
        cost_estimate=brief,
    )(*pieces)


def add_rows_kernel(whole_ref, got_ref, out_ref):
    total = whole_ref[...].astype(wide) + got_ref[...].astype(wide)
    out_ref[...] = total.astype(out_ref.dtype)


def add_rows(whole, place, got, kind):
    rows, columns = got.shape
    block = min(columns, 1024)
    part = pl.BlockSpec((rows, block), lambda j: (0, j))
    return call(
        add_rows_kernel,
        (columns // block,),
        in_specs=[pl.BlockSpec((rows, block), lambda j: (place, j)), part],
        out_specs=part,
        out_shape=jax.ShapeDtypeStruct(got.shape, kind),
    )(whole, got)


def split_kernel(rows, bits, *refs):
    ins, outs = refs[:4], refs[4:]
    for k in range(2):
        kept, got = ins[2 * k : 2 * k + 2]
        total = kept[...].astype(wide) + got[...].astype(wide)
        if bits is None:
            outs[k][...] = total
        else:
            taken = [0, 0]
            for i, side in enumerate(bits[k]):
                place = pl.ds(taken[side] * rows, rows)
                outs[2 * k + side][place, :] = total[i * rows : (i + 1) * rows].astype(low)
                taken[side] += 1


def split(kept, got, rows, bits):
    size, columns = kept[0].shape
    block = 512 if columns % 512 == 0 else 256
    part = pl.BlockSpec((size, block), lambda j: (0, j))
    half = pl.BlockSpec((size // 2, block), lambda j: (0, j))
    if bits is None:
        out_specs = [part] * 2
        out_shape = [jax.ShapeDtypeStruct((size, columns), wide)] * 2
    else:
        out_specs = [half] * 4
        out_shape = [jax.ShapeDtypeStruct((size // 2, columns), low)] * 4
    return call(
        functools.partial(split_kernel, rows, bits),
        (columns // block,),
        in_specs=[part] * 4,
        out_specs=out_specs,
        out_shape=out_shape,
    )(kept[0], got[0], kept[1], got[1])


def combine_kernel(heads, places, factor_ref, *refs):
    *piece_refs, total_ref = refs
    size = heads * KD // 2
    for part in range(2):
        for begin in range(0, size, KD // 2):
            h, row = divmod(part * size + begin, KD)
            rows = pl.ds(begin, KD // 2)
            total = jnp.zeros((KD // 2, VD), wide)
            for k, (operand, index) in enumerate(places[part][1:]):
                ref = piece_refs[operand]
                piece = ref[rows, :] if index is None else ref[index, rows, :]
                total = total + factor_ref[k * heads + h] * piece.astype(wide)
            total_ref[h, pl.ds(row, KD // 2), :] = total


def combine(gather, log_rate, length, backward):
    count = lax.axis_size("sq")
    place = lax.axis_index("sq")
    heads = log_rate.shape[0]
    factors = []
    for slot in range(1, count):
        other = place ^ mask_of(slot, count)
        ahead = (other - place) if backward else (place - other)
        between = jnp.maximum(ahead - 1, 0).astype(wide) * length
        factors.append(jnp.where(ahead > 0, jnp.exp(log_rate * between), 0.0))
    operands, places = gather.refs()
    vmem = pl.BlockSpec(memory_space=pltpu.VMEM)
    return pl.pallas_call(
        functools.partial(combine_kernel, heads, places),
        in_specs=[smem] + [vmem] * len(operands),
        out_specs=vmem,
        out_shape=jax.ShapeDtypeStruct((heads, KD, VD), wide),
        compiler_params=pltpu.CompilerParams(vmem_limit_bytes=56 * 2**20),
        cost_estimate=brief,
    )(jnp.concatenate(factors), *operands)


def call(kernel, grid, **options):
    return pl.pallas_call(
        kernel,
        grid=grid,
        cost_estimate=brief,
        compiler_params=pltpu.CompilerParams(
            dimension_semantics=("arbitrary",) * len(grid), vmem_limit_bytes=20 * 2**20
        ),
        **options,
    )


def dot(left_side, right_side, left_dim=1, right_dim=0):
    return lax.dot_general(
        left_side,
        right_side,
        (((left_dim,), (right_dim,)), ((), ())),
        preferred_element_type=wide,
    )


smem = pl.BlockSpec(memory_space=pltpu.SMEM)


def reach_of(rate):
    place = lax.broadcasted_iota(jnp.int32, (CHUNK, 1), 0).astype(wide)
    return jnp.exp(rate * (place + 1.0))


def tail_of(rate):
    place = lax.broadcasted_iota(jnp.int32, (CHUNK, 1), 0).astype(wide)
    return jnp.exp(rate * (CHUNK - 1.0 - place))


def decay_of(rate):
    row = lax.broadcasted_iota(jnp.int32, (CHUNK, CHUNK), 0)
    column = lax.broadcasted_iota(jnp.int32, (CHUNK, CHUNK), 1)
    spacing = (row - column).astype(wide)
    return jnp.where(spacing >= 0, jnp.exp(rate * jnp.maximum(spacing, 0.0)), 0.0)


brief = pl.CostEstimate(flops=1, bytes_accessed=1, transcendentals=0)


def bring(copies):
    for copy in copies:
        copy.start()
    return copies


def bring_pieces(refs, places, whole, sems, first):
    rows = whole.shape[0] // len(places)
    return bring(
        [
            pltpu.make_async_copy(
                refs[operand] if index is None else refs[operand].at[index],
                whole.at[pl.ds(k * rows, rows), :],
                sems.at[first + k],
            )
            for k, (operand, index) in enumerate(places)
        ]
    )


def wait_all(copies):
    for copy in copies:
        copy.wait()


def project_blocks(left, weight, product_ref):
    block = 256

    def one(j, carry):
        columns = pl.ds(pl.multiple_of(j * block, block), block)
        product_ref[:, columns] = dot(left[...], weight[:, columns]).astype(low)
        return carry

    lax.fori_loop(0, product_ref.shape[1] // block, one, 0)


def norm_project_kernel(count, slots, places, order, start, *refs):
    row_refs = refs[:slots]
    norm_ref = refs[slots]
    piece_refs = refs[slots + 1 : -8]
    normed_ref, xhat_ref, product_ref, full_ref, weight, normed, xhat, sems = refs[-8:]
    width = normed.shape[1] // count
    size = row_refs[0].shape[0]
    tile = 64
    copies = bring_pieces(piece_refs, places, weight, sems, 0)
    for turn, ref in enumerate(row_refs):

        def tile_of(t, carry, ref=ref, turn=turn):
            rows = pl.ds(pl.multiple_of(t * tile, tile), tile)
            values = [
                ref[rows, pl.ds(pl.multiple_of(order[s] * width, width), width)].astype(wide)
                for s in range(count)
            ]
            total = values[0]
            for v in values[1:]:
                total = total + v
            mean = jnp.sum(total, axis=1, keepdims=True) / (count * width)
            values = [v - mean for v in values]
            square = values[0] * values[0]
            for v in values[1:]:
                square = square + v * v
            square = jnp.sum(square, axis=1, keepdims=True)
            spread = lax.rsqrt(square / (count * width) + eps_layer)
            target = pl.ds(pl.multiple_of(start[turn] + t * tile, tile), tile)
            for s in range(count):
                columns = pl.ds(s * width, width)
                scaled = values[s] * spread
                xhat[target, columns] = scaled.astype(low)
                normed[target, columns] = (
                    scaled * norm_ref[0:1, columns] + norm_ref[1:2, columns]
                ).astype(low)
            return carry

        lax.fori_loop(0, size // tile, tile_of, 0)

    away = bring(
        [
            pltpu.make_async_copy(normed, normed_ref, sems.at[count]),
            pltpu.make_async_copy(xhat, xhat_ref, sems.at[count + 1]),
        ]
    )
    wait_all(copies)
    away += bring([pltpu.make_async_copy(weight, full_ref, sems.at[count + 2])])
    project_blocks(normed, weight, product_ref)
    wait_all(away)


def norm_project(slots, norms, gather, columns, order, start):
    count = gather.count
    pieces, places = gather.refs()
    size, depth = slots[0].shape
    length = size * len(slots)
    width = pieces[0].shape[1]
    vmem = pl.BlockSpec(memory_space=pltpu.VMEM)
    whole = pl.BlockSpec(memory_space=pl.ANY)
    return pl.pallas_call(
        functools.partial(norm_project_kernel, count, len(slots), places[0]),
        in_specs=[smem, smem] + [vmem] * (len(slots) + 1) + [whole] * len(pieces),
        out_specs=[whole, whole, vmem, whole],
        out_shape=[
            jax.ShapeDtypeStruct((length, depth), low),
            jax.ShapeDtypeStruct((length, depth), low),
            jax.ShapeDtypeStruct((length, columns), low),
            jax.ShapeDtypeStruct((depth, width), low),
        ],
        scratch_shapes=[
            pltpu.VMEM((depth, width), low),
            pltpu.VMEM((length, depth), low),
            pltpu.VMEM((length, depth), low),
            pltpu.SemaphoreType.DMA((count + 3,)),
        ],
        compiler_params=pltpu.CompilerParams(vmem_limit_bytes=36 * 2**20),
        cost_estimate=brief,
    )(order, start, *slots, norms, *pieces)


def project_kernel(count, places, left_ref, *refs):
    product_ref, full_ref, weight, sems = refs[-4:]
    wait_all(bring_pieces(refs[:-4], places, weight, sems, 0))
    away = bring([pltpu.make_async_copy(weight, full_ref, sems.at[count])])
    project_blocks(left_ref, weight, product_ref)
    wait_all(away)


def project_pieces(left_side, gather, columns):
    length, depth = left_side.shape
    count = gather.count
    pieces, places = gather.refs()
    width = pieces[0].shape[1]
    vmem = pl.BlockSpec(memory_space=pltpu.VMEM)
    whole = pl.BlockSpec(memory_space=pl.ANY)
    return pl.pallas_call(
        functools.partial(project_kernel, count, places[1]),
        in_specs=[vmem] + [whole] * len(pieces),
        out_specs=[vmem, whole],
        out_shape=[
            jax.ShapeDtypeStruct((length, columns), low),
            jax.ShapeDtypeStruct((depth, width), low),
        ],
        scratch_shapes=[pltpu.VMEM((depth, width), low), pltpu.SemaphoreType.DMA((count + 1,))],
        compiler_params=pltpu.CompilerParams(vmem_limit_bytes=20 * 2**20),
        cost_estimate=brief,
    )(left_side, *pieces)


def feed_kernel(top, quarter, places, sizes, has_prior, second_ref, cot_ref, *refs):
    quarters = len(places)
    piece_refs = []
    for size in sizes:
        piece_refs.append(refs[:size])
        refs = refs[size:]
    if has_prior:
        prior_grad, prior_down, *refs = refs
    hidden_refs = [refs[2 * t : 2 * t + 2] for t in range(quarters)]
    grad_ref, down_part_ref = refs[2 * quarters : 2 * quarters + 2]
    first, later, gate_pre, up_pre, grad_inner, sums, sems = refs[2 * quarters + 2 :]
    rows, depth = second_ref.shape
    middle = quarter // 2
    hidden = pl.ds(0, quarter)
    hidden_up = pl.ds(quarter, quarter)
    down = pl.ds(quarter, middle)
    sides = [pl.ds(0, middle), pl.ds(middle, middle)]
    halves = [pl.ds(0, depth // 2), pl.ds(depth // 2, depth // 2)]
    copies = []
    for t in range(quarters):
        for k, whole in enumerate((first, later)):
            index = (t * 2 + k) * 2 * top
            some = bring_pieces(piece_refs[t], places[t][k], whole.at[t], sems, index)
            copies += [some[:top], some[top:]]
    tile = 16
    scale = 0.7978845608028654
    for t in range(quarters):
        inner_ref, grads_ref = hidden_refs[t]
        for k, (whole, target) in enumerate(((first, gate_pre), (later, up_pre))):
            for h in range(2):
                wait_all(copies[(t * 2 + k) * 2 + h])
                part = dot(second_ref[:, halves[h]], whole[t, halves[h], hidden])
                side = dot(cot_ref[:, halves[h]], whole[t, halves[h], down])
                target[...] = part if h == 0 else target[...] + part
                grad_inner[:, sides[k]] = side if h == 0 else grad_inner[:, sides[k]] + side

        def activate(i, carry, inner_ref=inner_ref, grads_ref=grads_ref):
            at = pl.ds(pl.multiple_of(i * tile, tile), tile)
            v, u, g = gate_pre[at, :], up_pre[at, :], grad_inner[at, :]
            square = v * v
            bent = jnp.tanh(scale * v * (1.0 + 0.044715 * square))
            shared = 0.5 * (1.0 + bent)
            gelu = v * shared
            slope = shared + (0.5 * scale) * v * (1.0 - bent * bent) * (1.0 + 0.134145 * square)
            inner_ref[at, :] = (gelu * u).astype(low)
            grads_ref[at, hidden] = (g * u * slope).astype(low)
            grads_ref[at, hidden_up] = (g * gelu).astype(low)
            return carry

        lax.fori_loop(0, rows // tile, activate, 0)
        for half in halves:
            grad = dot(grads_ref[:, hidden], first[t, half, hidden], 1, 1)
            grad = grad + dot(grads_ref[:, hidden_up], later[t, half, hidden], 1, 1)
            down_part = dot(inner_ref[:, sides[0]], first[t, half, down], 1, 1)
            down_part = down_part + dot(inner_ref[:, sides[1]], later[t, half, down], 1, 1)
            if t > 0:
                grad = grad + sums[0, :, half]
                down_part = down_part + sums[1, :, half]
            elif has_prior:
                grad = grad + prior_grad[:, half]
                down_part = down_part + prior_down[:, half]
            if t < quarters - 1:
                sums[0, :, half] = grad
                sums[1, :, half] = down_part
            else:
                grad_ref[:, half] = grad.astype(grad_ref.dtype)
                down_part_ref[:, half] = down_part.astype(down_part_ref.dtype)


def feed_part(second, cot, gathers, quarter, prior, kind):
    top = gathers[0].top
    quarters = len(gathers)
    rows, depth = second.shape
    pieces, places, sizes = [], [], []
    for gather in gathers:
        operands, where = gather.refs()
        pieces += operands
        places.append(where)
        sizes.append(len(operands))
    width = pieces[0].shape[1]
    vmem = pl.BlockSpec(memory_space=pltpu.VMEM)
    out = jax.ShapeDtypeStruct((rows, depth), kind)
    hidden = [
        jax.ShapeDtypeStruct((rows, quarter), low),
        jax.ShapeDtypeStruct((rows, 2 * quarter), low),
    ]
    return pl.pallas_call(
        functools.partial(feed_kernel, top, quarter, places, sizes, bool(prior)),
        in_specs=[vmem] * 2
        + [pl.BlockSpec(memory_space=pl.ANY)] * len(pieces)
        + [vmem] * len(prior),
        out_specs=[vmem] * (2 * quarters + 2),
        out_shape=hidden * quarters + [out, out],
        scratch_shapes=[
            pltpu.VMEM((quarters, depth, width), low),
            pltpu.VMEM((quarters, depth, width), low),
            pltpu.VMEM((rows, quarter), wide),
            pltpu.VMEM((rows, quarter), wide),
            pltpu.VMEM((rows, quarter), wide),
            pltpu.VMEM((2, rows, depth), wide),
            pltpu.SemaphoreType.DMA((4 * top * quarters,)),
        ],
        compiler_params=pltpu.CompilerParams(vmem_limit_bytes=(22 + 12 * quarters) * 2**20),
        cost_estimate=brief,
    )(second, cot, *pieces, *prior)


def outer_kernel(count, added, rows, bits, *refs):
    lefts, rights, refs = refs[:count], refs[count : 2 * count], refs[2 * count :]
    got = refs[0] if added else None
    outs, flipped = refs[added:-1], refs[-1]
    turn = pl.program_id(0)
    starts = [sum(ref.shape[0] for ref in lefts[:i]) for i in range(count)]

    @pl.when(turn == 0)
    def _():
        for begin, ref in zip(starts, lefts):
            flipped[:, pl.ds(begin, ref.shape[0])] = ref[...].T

    total = 0.0
    for begin, ref in zip(starts, rights):
        total = total + dot(flipped[:, pl.ds(begin, ref.shape[0])], ref[...])
    if added:
        total = total + got[...].astype(wide)
    if bits is None:
        outs[0][...] = total.astype(low)
    else:
        for k in range(2):

            @pl.when(turn // (pl.num_programs(0) // 2) == k)
            def _(k=k):
                taken = [0, 0]
                for i, side in enumerate(bits[k]):
                    place = pl.ds(taken[side] * rows, rows)
                    outs[2 * k + side][place, :] = total[i * rows : (i + 1) * rows].astype(low)
                    taken[side] += 1


def outer_half(lefts, rights, part, got=None, rows=None, bits=None):
    depth = lefts[0].shape[1] // 2
    columns = rights[0].shape[1]
    block = 512 if columns % 1024 == 0 else 256
    blocks = columns // block
    whole = pl.BlockSpec((depth, block), lambda j: (0, j))
    extra = [] if got is None else [got]
    if bits is None:
        out_specs, out_shape = [whole], [jax.ShapeDtypeStruct((depth, columns), low)]
    else:
        early = pl.BlockSpec((depth // 2, block), lambda j: (0, jnp.minimum(j, blocks // 2 - 1)))
        late = pl.BlockSpec((depth // 2, block), lambda j: (0, jnp.maximum(j - blocks // 2, 0)))
        out_specs = [early, early, late, late]
        out_shape = [jax.ShapeDtypeStruct((depth // 2, columns // 2), low)] * 4
    result = call(
        functools.partial(outer_kernel, len(lefts), len(extra), rows, bits),
        (blocks,),
        in_specs=[pl.BlockSpec((v.shape[0], depth), lambda j: (0, part)) for v in lefts]
        + [pl.BlockSpec((v.shape[0], block), lambda j: (0, j)) for v in rights]
        + [whole] * len(extra),
        out_specs=out_specs,
        out_shape=out_shape,
        scratch_shapes=[pltpu.VMEM((depth, sum(v.shape[0] for v in lefts)), low)],
    )(*lefts, *rights, *extra)
    return result[0] if bits is None else list(result)


def rows_kernel(parts, sides, sums, size, begin_ref, *refs):
    lefts = [refs[p * sides : (p + 1) * sides] for p in range(parts)]
    refs = refs[parts * sides :]
    xhats, weights, out_ref = refs[: parts * sums], refs[parts * sums :][:sides], refs[parts * sums + sides]
    for p in range(parts):
        part = dot(lefts[p][0][...], weights[0][...], 1, 1)
        for k in range(1, sides):
            part = part + dot(lefts[p][k][...], weights[k][...], 1, 1)
        out_ref[pl.ds(p * size, size), :] = part.astype(out_ref.dtype)
        if sums:
            sums_ref = refs[-1]
            gain = jnp.sum(part * xhats[p][...].astype(wide), axis=0, keepdims=True)
            shift = jnp.sum(part, axis=0, keepdims=True)
            sums_ref[0:1, :] = gain if p == 0 else sums_ref[0:1, :] + gain
            sums_ref[1:2, :] = shift if p == 0 else sums_ref[1:2, :] + shift


def rows_back(lefts, weights, begins, size, xhat=None):
    depth = weights[0][0].shape[0]
    block = 512
    parts, sides = len(begins), len(lefts)
    in_specs, operands = [], []
    for p in range(parts):
        for (left, column), (_, _, columns) in zip(lefts, weights):
            in_specs.append(pl.BlockSpec((size, columns), lambda j, b, p=p, column=column: (b[p], column)))
            operands.append(left)
    if xhat is not None:
        for p in range(parts):
            in_specs.append(pl.BlockSpec((size, block), lambda j, b, p=p: (b[p], j)))
            operands.append(xhat)
    for weight, column, columns in weights:
        in_specs.append(pl.BlockSpec((block, columns), lambda j, b, column=column: (j, column)))
        operands.append(weight)
    out_specs = [pl.BlockSpec((parts * size, block), lambda j, b: (0, j))]
    out_shape = [jax.ShapeDtypeStruct((parts * size, depth), low)]
    if xhat is not None:
        out_specs.append(pl.BlockSpec((2, block), lambda j, b: (0, j)))
        out_shape.append(jax.ShapeDtypeStruct((2, depth), wide))
    return pl.pallas_call(
        functools.partial(rows_kernel, parts, sides, int(xhat is not None), size),
        grid_spec=pltpu.PrefetchScalarGridSpec(
            num_scalar_prefetch=1, grid=(depth // block,), in_specs=in_specs, out_specs=out_specs
        ),
        out_shape=out_shape,
        compiler_params=pltpu.CompilerParams(vmem_limit_bytes=56 * 2**20),
        cost_estimate=brief,
    )(jnp.stack(begins) // size, *operands)


def parts_of(heads):
    values = [pl.ds(h * VD, VD) for h in range(heads)]
    keys = [pl.ds(heads * VD + h * KD, KD) for h in range(heads)]
    return values, keys


def state_halves(state, heads, refs):
    if heads == 2:
        for h in range(2):
            refs[h][...] = state[h].astype(low)
    else:
        for k in range(2):
            refs[k][...] = state[0, pl.ds(k * KD // 2, KD // 2), :].astype(low)


def state_kernel(heads, chunks, rate_ref, kv_ref, one_ref, two_ref, state):
    values, keys = parts_of(heads)
    turn = pl.program_id(0)

    @pl.when(turn == 0)
    def _():
        state[...] = jnp.zeros_like(state)

    for h in range(heads):
        rate = rate_ref[h]
        scaled = (kv_ref[:, keys[h]].astype(wide) * tail_of(rate)).astype(low)
        kept = state[h] * jnp.exp(jnp.full((1, 1), rate * CHUNK, wide))
        state[h] = kept + dot(scaled, kv_ref[:, values[h]], 0, 0)

    @pl.when(turn == chunks - 1)
    def _():
        state_halves(state, heads, [one_ref, two_ref])


def final_state(kv, log_rate, heads):
    length, columns = kv.shape
    chunks = length // CHUNK
    half = jax.ShapeDtypeStruct((heads * KD // 2, VD), low)
    return call(
        functools.partial(state_kernel, heads, chunks),
        (chunks,),
        in_specs=[smem, pl.BlockSpec((CHUNK, columns), lambda c: (c, 0))],
        out_specs=[pl.BlockSpec(half.shape, lambda c: (0, 0))] * 2,
        out_shape=[half, half],
        scratch_shapes=[pltpu.VMEM((heads, KD, VD), wide)],
    )(log_rate, kv)


def retain_kernel(
    heads, rate_ref, kv_ref, qs_ref, first_ref, gated_ref, grouped_ref, factor_ref, states_ref, held, table
):
    values, keys = parts_of(heads)

    @pl.when(pl.program_id(0) == 0)
    def _():
        held[...] = first_ref[...]
        for h in range(heads):
            table[h] = decay_of(rate_ref[h])

    for h in range(heads):
        rate = rate_ref[h]
        query, key = qs_ref[:, keys[h]], kv_ref[:, keys[h]]
        value = kv_ref[:, values[h]]
        state = held[h]
        state_low = state.astype(low)
        states_ref[0, h] = state_low
        mixing = (dot(query, key, 1, 1) * table[h]).astype(low)
        retained = dot(mixing, value) + reach_of(rate) * dot(query, state_low)
        scaled = (key.astype(wide) * tail_of(rate)).astype(low)
        held[h] = state * jnp.exp(jnp.full((1, 1), rate * CHUNK, wide)) + dot(scaled, value, 0, 0)
        factor = lax.rsqrt(jnp.mean(retained * retained, axis=1, keepdims=True) + eps_group)
        grouped = (retained * factor).astype(low)
        factor_ref[h] = factor
        grouped_ref[:, values[h]] = grouped
        pre = qs_ref[:, values[h]].astype(wide)
        gated_ref[:, values[h]] = (grouped.astype(wide) * (pre * jax.nn.sigmoid(pre))).astype(low)


def retain(kv, qs, first, log_rate, heads):
    length, columns = kv.shape
    chunks = length // CHUNK
    rows = pl.BlockSpec((CHUNK, columns), lambda c: (c, 0))
    out = pl.BlockSpec((CHUNK, heads * VD), lambda c: (c, 0))
    return call(
        functools.partial(retain_kernel, heads),
        (chunks,),
        in_specs=[smem, rows, rows, pl.BlockSpec((heads, KD, VD), lambda c: (0, 0, 0))],
        out_specs=[
            out,
            out,
            pl.BlockSpec((heads, CHUNK, 1), lambda c: (0, c, 0)),
            pl.BlockSpec((1, heads, KD, VD), lambda c: (c, 0, 0, 0)),
        ],
        out_shape=[
            jax.ShapeDtypeStruct((length, heads * VD), low),
            jax.ShapeDtypeStruct((length, heads * VD), low),
            jax.ShapeDtypeStruct((heads, length, 1), wide),
            jax.ShapeDtypeStruct((chunks, heads, KD, VD), low),
        ],
        scratch_shapes=[pltpu.VMEM((heads, KD, VD), wide), pltpu.VMEM((heads, CHUNK, CHUNK), wide)],
    )(log_rate, kv, qs, first)


def gate_back_kernel(
    heads, first, last, place_ref, rate_ref, branch_ref, left_ref, right_ref, grouped_ref, factor_ref, qs_ref, *refs
):
    values, keys = parts_of(heads)
    if not first:
        _, _, prior_ref, *refs = refs
    swish_ref, retained_ref, *halves, crossed_ref = refs
    start = (place_ref[0] * CHUNK).astype(wide)
    sides = [dot(branch_ref[...], ref[...]) for ref in (left_ref, right_ref)]
    gated = sides if heads == 2 else [jnp.concatenate(sides, axis=1)]
    for h in range(heads):
        rate = rate_ref[h]
        gated_grad = gated[h]
        grouped = grouped_ref[:, values[h]].astype(wide)
        pre = qs_ref[:, values[h]].astype(wide)
        sigma = jax.nn.sigmoid(pre)
        swish_ref[:, values[h]] = (
            gated_grad * grouped * (sigma * (1.0 + pre * (1.0 - sigma)))
        ).astype(low)
        grouped_grad = (gated_grad * (pre * sigma)).astype(low).astype(wide)
        factor = factor_ref[h]
        mean = jnp.mean(grouped_grad * grouped, axis=1, keepdims=True)
        retained_grad = (factor * (grouped_grad - grouped * mean)).astype(low)
        retained_ref[:, values[h]] = retained_grad
        scale = reach_of(rate) * jnp.exp(jnp.full((1, 1), rate * start, wide))
        scaled = (qs_ref[:, keys[h]].astype(wide) * scale).astype(low)
        crossed = dot(scaled, retained_grad, 0, 0)
        crossed_ref[h] = crossed if first else prior_ref[h] + crossed
    if last:
        state_halves(crossed_ref, heads, halves)


def gate_back(branch, left, right, column, grouped, factor, qs, log_rate, heads, place, prior, last):
    length, columns = qs.shape
    depth = branch.shape[1]
    part = pl.BlockSpec((CHUNK, heads * VD), lambda i, p: (p[0], 0))
    total = pl.BlockSpec((heads, KD, VD), lambda i, p: (0, 0, 0))
    whole = pl.BlockSpec(memory_space=pl.ANY)
    half = pl.BlockSpec((heads * KD // 2, VD), lambda i, p: (0, 0))
    grid_spec = pltpu.PrefetchScalarGridSpec(
        num_scalar_prefetch=1,
        grid=(1,),
        in_specs=[
            smem,
            pl.BlockSpec((CHUNK, depth), lambda i, p: (0, 0)),
            pl.BlockSpec((depth, heads * VD // 2), lambda i, p: (0, column)),
            pl.BlockSpec((depth, heads * VD // 2), lambda i, p: (0, column)),
            part,
            pl.BlockSpec((heads, CHUNK, 1), lambda i, p: (0, p[0], 0)),
            pl.BlockSpec((CHUNK, columns), lambda i, p: (p[0], 0)),
        ]
        + [whole, whole, total][: len(prior)],
        out_specs=[part, part] + ([half] * 2 if last else [total]),
        scratch_shapes=[pltpu.VMEM((heads, KD, VD), wide)] if last else [],
    )
    return pl.pallas_call(
        functools.partial(gate_back_kernel, heads, not prior, last),
        grid_spec=grid_spec,
        out_shape=[
            jax.ShapeDtypeStruct((length, heads * VD), low),
            jax.ShapeDtypeStruct((length, heads * VD), low),
        ]
        + (
            [jax.ShapeDtypeStruct((heads * KD // 2, VD), low)] * 2
            if last
            else [jax.ShapeDtypeStruct((heads, KD, VD), wide)]
        ),
        input_output_aliases={8: 0, 9: 1} if prior else {},
        compiler_params=pltpu.CompilerParams(vmem_limit_bytes=56 * 2**20),
        cost_estimate=brief,
    )(place.reshape(1), log_rate, branch, left, right, grouped, factor, qs, *prior)


def retain_back_kernel(
    heads, rate_ref, kv_ref, qs_ref, grad_ref, states_ref, last_ref, back_ref, held, table
):
    values, keys = parts_of(heads)
    queries = [pl.ds(heads * (VD + KD) + h * KD, KD) for h in range(heads)]

    @pl.when(pl.program_id(0) == 0)
    def _():
        held[...] = last_ref[...]
        for h in range(heads):
            table[h] = decay_of(rate_ref[h])

    for h in range(heads):
        rate = rate_ref[h]
        query, key = qs_ref[:, keys[h]], kv_ref[:, keys[h]]
        value, grad = kv_ref[:, values[h]], grad_ref[:, values[h]]
        decay = table[h]
        reach, tail = reach_of(rate), tail_of(rate)
        later = held[h]
        later_low = later.astype(low)
        mixing = (dot(query, key, 1, 1) * decay).astype(low)
        scores_grad = (dot(grad, value, 1, 1) * decay).astype(low)
        back_ref[:, queries[h]] = (
            dot(scores_grad, key) + reach * dot(grad, states_ref[0, h], 1, 1)
        ).astype(low)
        back_ref[:, keys[h]] = (
            dot(scores_grad, query, 0, 0) + tail * dot(value, later_low, 1, 1)
        ).astype(low)
        back_ref[:, values[h]] = (
            dot(mixing, grad, 0, 0) + tail * dot(key, later_low)
        ).astype(low)
        scaled = (query.astype(wide) * reach).astype(low)
        held[h] = later * jnp.exp(jnp.full((1, 1), rate * CHUNK, wide)) + dot(scaled, grad, 0, 0)


def retain_back(kv, qs, retained_grad, states, last, log_rate, heads):
    length, columns = kv.shape
    chunks = length // CHUNK
    rows = pl.BlockSpec((CHUNK, columns), lambda c: (chunks - 1 - c, 0))
    part = pl.BlockSpec((CHUNK, heads * VD), lambda c: (chunks - 1 - c, 0))
    return call(
        functools.partial(retain_back_kernel, heads),
        (chunks,),
        in_specs=[
            smem,
            rows,
            rows,
            part,
            pl.BlockSpec((1, heads, KD, VD), lambda c: (chunks - 1 - c, 0, 0, 0)),
            pl.BlockSpec((heads, KD, VD), lambda c: (0, 0, 0)),
        ],
        out_specs=pl.BlockSpec((CHUNK, columns + heads * KD), lambda c: (chunks - 1 - c, 0)),
        out_shape=jax.ShapeDtypeStruct((length, columns + heads * KD), low),
        scratch_shapes=[pltpu.VMEM((heads, KD, VD), wide), pltpu.VMEM((heads, CHUNK, CHUNK), wide)],
    )(log_rate, kv, qs, retained_grad, states, last)


def shards(
    layer_in,
    norm1_gain,
    norm1_bias,
    w_query,
    w_key,
    w_value,
    w_swish,
    w_out,
    norm2_gain,
    norm2_bias,
    w_gate,
    w_up,
    w_down,
    cotangent,
):
    count_sq = lax.axis_size("sq")
    count_head = lax.axis_size("head")
    sq_index = lax.axis_index("sq")
    head_index = lax.axis_index("head")
    own_rows = layer_in.shape[0]
    length = own_rows * count_head
    key_scale = KD ** (-0.5)
    value_width = w_value.shape[1]
    depth = layer_in.shape[1]
    heads = value_width // VD
    log_rate = log_decay(head_index * heads, heads)
    order = jnp.stack([sq_index ^ mask_of(s, count_sq) for s in range(count_sq)]).astype(jnp.int32)
    start = [lax.rem(head_index - t + count_head, count_head) * own_rows for t in range(count_head)]
    kin_steps = []
    while 2 << len(kin_steps) < count_head:
        kin_steps.append(2 << len(kin_steps))

    key_width = w_key.shape[1]
    pair_width = value_width + key_width

    norm = Small(jnp.stack([norm1_gain, norm1_bias, norm2_gain, norm2_bias]))
    out_shard = w_out.T
    out_half = out_shard.shape[1] // 2
    first = Gather(
        jnp.concatenate(
            [w_value, (w_key.astype(wide) * key_scale).astype(low), out_shard[:, :out_half]], axis=1
        ),
        jnp.concatenate([w_swish, w_query, out_shard[:, out_half:]], axis=1),
    )
    quarter_width = w_gate.shape[1]
    middle = quarter_width // 2
    down_shard = w_down.T
    feed_first = Box(jnp.concatenate([w_gate, down_shard[:, :middle]], axis=1))
    feed_later = Box(jnp.concatenate([w_up, down_shard[:, middle:]], axis=1))
    cot_own = Box(own_order(cotangent))
    x_own = Box(own_order(layer_in))
    slots = [Box(layer_in)]
    settle(slots[0], first, norm)
    for turn in range(1, count_head):
        slots.append(Box(ring_step(slots[-1].value)))
        first.core()
        first.send()
        norm.send()
        settle(slots[-1], first, norm, feed_first, feed_later, cot_own, x_own)
    norm.rest()
    first.rest()
    first.core()

    def kin(value):
        held = [value]
        for step in kin_steps:
            held += [swap_head(v, step) for v in held]
        return held

    x_own = x_own.value
    kin_parts = [
        Box(feed_first.value[:, :quarter_width]),
        Box(feed_later.value[:, :quarter_width]),
        Box(jnp.concatenate([v.value[:, quarter_width:] for v in (feed_first, feed_later)], axis=1)),
    ]
    packs = [Many(*kin(kin_parts[0].value)[1:])]
    cot_far = Box(swap_head(cot_own.value, 1))
    feeds = [Gather(feed_first.value, feed_later.value)]
    feeds[0].send()
    norms = jnp.concatenate([norm.pieces[s] for s in range(count_sq)], axis=1).astype(wide)
    gain_one, shift_one, gain_two, shift_two = norms[0], norms[1], norms[2], norms[3]
    normed, xhat, kv, first_full = norm_project(
        [b.value for b in slots],
        norms,
        first,
        pair_width,
        order,
        jnp.stack(start).astype(jnp.int32),
    )
    passed = Gather(*final_state(kv, log_rate, heads))
    settle(passed, *packs, cot_far, feeds[0], cot_own, *kin_parts[1:])

    passed.send()
    packs.append(Many(*kin(kin_parts[1].value)[1:]))
    settle(passed)
    passed.rest()
    qs, later_full = project_pieces(normed, first, pair_width)
    qs = Box(qs)
    settle(passed, packs[1], cot_far, feeds[0], cot_own, kin_parts[2], qs)
    qs, cot_own = qs.value, cot_own.value
    passed.core()
    packs.append(Many(*kin(kin_parts[2].value)[1:]))
    feeds[0].core()
    feeds[0].send()
    incoming = combine(passed, log_rate, length, False)
    gated_low, grouped, factor, states = retain(kv, qs, incoming, log_rate, heads)

    out_column = pair_width // out_half

    def out_part(turns):
        (parts,) = rows_back(
            [(gated_low, 0), (gated_low, 1)],
            [(first_full, out_column, out_half), (later_full, out_column, out_half)],
            [start[turn % count_head] for turn in turns],
            own_rows,
        )
        return parts

    total = Box(out_part([1]))
    gated = Box(gated_low)
    settle(total, feeds[0], packs[2], gated)
    gated_low = gated.value
    quarters = 1 + len(packs[0].value)
    parts = Box(out_part(range(2, count_head + 1)))
    for turn in range(2, count_head + 1):
        got = ring_step(total.value)
        feeds[0].core()
        if turn == 2:
            feeds[0].send()
            feeds += [
                Gather(
                    jnp.concatenate([gate, down[:, :middle]], axis=1),
                    jnp.concatenate([up, down[:, middle:]], axis=1),
                )
                for gate, up, down in zip(*[p.value for p in packs])
            ]
        else:
            for thing in feeds[1:]:
                thing.core()
                thing.send()
        total = Box(add_rows(parts.value, turn - 2, got, low if turn < count_head else wide))
        settle(total, *feeds, parts)
    hidden = x_own.astype(wide) + total.value
    second_own = Box(layer_norm(hidden, gain_two, shift_two).astype(low))

    settle(second_own, *feeds)
    second_own = second_own.value
    second_far = Box(swap_head(second_own, 1))
    for thing in feeds:
        thing.core()
        thing.rest()
    feeds[0].core()
    fed = feed_part(second_own, cot_own, feeds[:1], quarter_width, [], wide)
    inner_own, grads_own, fed_sums = [fed[0]], [fed[1]], Many(*fed[2:])
    settle(second_far, *feeds[1:], cot_far, fed_sums)
    second_far, cot_far = second_far.value, cot_far.value
    for thing in feeds[1:]:
        thing.core()
    fed = feed_part(second_far, cot_far, feeds, quarter_width, [], low)
    inner_far, grads_far = fed[: 2 * quarters : 2], fed[1 : 2 * quarters : 2]
    grad_far, down_far, near = Box(fed[-2]), Box(fed[-1]), Box(second_own)
    settle(grad_far, near, down_far)

    grad_far = Box(swap_head(grad_far.value, 1))
    fed = feed_part(near.value, cot_own, feeds[1:], quarter_width, fed_sums.value, wide)
    inner_own += fed[: 2 * quarters - 2 : 2]
    grads_own += fed[1 : 2 * quarters - 2 : 2]
    second = Many(near.value, second_far)
    cot = Many(cot_own, cot_far)
    inner = Many(beside(inner_own), beside(inner_far))
    grads = [Many(a, b) for a, b in zip(grads_own, grads_far)]
    early_sum = Scatter(second.value, grads[0].value)
    early_sum.core()
    early_sum.near()
    late_sums = [Scatter(second.value, g.value) for g in grads[1:]]
    settle(grad_far, early_sum, *late_sums, cot, inner)
    second_grad = fed[-2] + grad_far.value.astype(wide)
    _, second_back = jax.vjp(layer_norm, hidden, gain_two, shift_two)
    hidden_part, gain_two_part, shift_two_part = second_back(second_grad)
    grad_hidden = cot_own.astype(wide) + hidden_part

    slots = [Box(grad_hidden.astype(low))]
    settle(slots[0], early_sum, *late_sums, cot, inner)
    passing = []
    for turn in range(count_head):
        rows = slots[-1]
        if turn < count_head - 1:
            slots.append(Box(ring_step(rows.value)))
        if turn == 0:
            early_sum.send(True)
            for thing in late_sums:
                thing.core()
                thing.near()
            down_sum = Scatter(cot.value, inner.value)
            waits = [early_sum, *late_sums, down_sum]
        elif turn == 1:
            for thing in late_sums:
                thing.send()
            down_sum.core()
            down_sum.near()
        elif turn == 2:
            for thing in late_sums:
                thing.rest()
            down_sum.send()
        passing = gate_back(
            rows.value,
            first_full,
            later_full,
            out_column,
            grouped,
            factor,
            qs,
            log_rate,
            heads,
            start[turn] // own_rows,
            passing,
            turn == count_head - 1,
        )
        if turn < count_head - 1:
            passing = Many(*passing)
            settle(slots[-1], *waits, cot, inner, passing)
            passing = passing.value
    swish_grad, retained_grad, *crossed = passing

    def kin_sum(held):
        parts = []
        held = [None] + list(held)
        for step in kin_steps[::-1]:
            size = len(held) // 2
            got = [swap_head(h, step) for h in held[size:]]
            parts.append(got[0])
            held = [None] + [
                (h.astype(wide) + g.astype(wide)).astype(low) for h, g in zip(held[1:size], got[1:])
            ]
        return parts

    branch_low = jnp.zeros((length, depth), low)
    for turn, rows in enumerate(slots):
        branch_low = lax.dynamic_update_slice_in_dim(branch_low, rows.value, start[turn], 0)
    branch, gated = Box(branch_low), Box(gated_low)
    ups = [thing.rest()[1].astype(low) for thing in late_sums]
    early = [
        Many(
            *kin_sum(
                [
                    jnp.concatenate([thing.rest()[0].astype(low), up[:, :middle]], axis=1)
                    for thing, up in zip(late_sums, ups)
                ]
            )
        )
    ]
    ups = Many(*[up[:, middle:] for up in ups])
    passed = Gather(*crossed)
    swish = Box(swish_grad)
    settle(passed, early_sum, down_sum, ups, branch, gated, swish)
    passed.send()
    settle(passed, down_sum, ups, swish)
    passed.rest()
    down_sum.rest()
    swish_sum = Scatter([normed], [swish.value])
    settle(passed, early[0], early_sum, down_sum, ups, swish_sum)
    passed.core()
    down_parts = jnp.split(jnp.concatenate(down_sum.rest(), axis=1), quarters, axis=1)
    early.append(
        Many(
            *kin_sum(
                [
                    jnp.concatenate([up, part.astype(low)], axis=1)
                    for up, part in zip(ups.value, down_parts[1:])
                ]
            )
        )
    )
    early_sum.send(True)
    swish_sum.core()
    returned = combine(passed, log_rate, length, True)
    backs = retain_back(kv, qs, retained_grad, states, returned, log_rate, heads)

    def normed_part(turns, backs):
        query = 2 + value_width // key_width - 1
        return rows_back(
            [(backs, 0), (swish_grad, 0), (backs, query)],
            [
                (first_full, 0, pair_width),
                (later_full, 0, value_width),
                (later_full, query - 1, key_width),
            ],
            [start[turn % count_head] for turn in turns],
            own_rows,
            xhat,
        )

    total, norm_sums = normed_part([1], backs)
    total, backs, norm_sums = Box(total), Box(backs), Box(norm_sums)
    settle(total, early_sum, swish_sum, backs, norm_sums, branch, gated, down_far, early[1])
    parts, more_sums = normed_part(range(2, count_head + 1), backs.value)
    parts = Box(parts)
    more_sums = Box(more_sums)
    waits = [early_sum]
    for turn in range(2, count_head + 1):
        got = ring_step(total.value)
        if turn == 2:
            early_sum.rest()
            swish_sum.near()
            swish_sum.send(True)
            back_sum = Scatter([normed], [backs.value])
            back_sum.core()
            back_sum.near()
            waits = [early_sum, swish_sum, back_sum, more_sums]
        elif turn == 3:
            back_sum.send()
            out_sum = Scatter([branch.value], [gated.value])
            out_sum.core()
            out_sum.near()
            waits = [swish_sum, back_sum, out_sum, more_sums]
        elif turn == 4:
            back_sum.rest()
            swish_sum.rest()
            norm_sums = norm_sums.value + more_sums.value
            norm_sums = true_order(
                jnp.concatenate([norm_sums, jnp.stack([gain_two_part, shift_two_part])])
            )
            norm_sums = Box(sum_others(norm_sums, "sq", [1]))
            waits = [back_sum, swish_sum, out_sum, norm_sums]
        total = Box(add_rows(parts.value, turn - 2, got, low if turn < count_head else wide))
        settle(total, *waits, parts, branch, gated, down_far)
    down_far = swap_head(down_far.value, 1)
    _, first_back = jax.vjp(lambda v: layer_norm(v, gain_one, shift_one), x_own.astype(wide))
    grad_in = grad_hidden + first_back(total.value)[0]
    norm_sums = sum_others(norm_sums.value, "sq", range(2, count_sq, 2))
    norm_sums = sum_others(norm_sums, "head", range(1, count_head))
    first_sum, later_sum = early_sum.rest()
    early = [sum(p.astype(wide) for p in e.value) for e in early]
    grad_gate = first_sum + early[0][:, :quarter_width]
    grad_up = later_sum + jnp.concatenate(
        [early[0][:, quarter_width:], early[1][:, :middle]], axis=1
    )
    grad_down = (down_parts[0] + early[1][:, middle:]).T
    grad_value, grad_key_query = back_sum.rest()
    grad_swish = jnp.concatenate(swish_sum.rest(), axis=1)
    grad_out = jnp.concatenate(out_sum.rest(), axis=1).T
    result = (hidden + fed[-1] + down_far.astype(wide)).astype(low)

    piece = depth // (count_sq * count_head)
    first_norm = lax.dynamic_slice_in_dim(
        norm_sums[:2], (head_index * count_sq + sq_index) * piece, piece, 1
    )
    piece = depth // count_sq
    second_norm = lax.dynamic_slice_in_dim(norm_sums[2:], sq_index * piece, piece, 1)
    return (
        true_order(result),
        true_order(grad_in),
        first_norm[0],
        first_norm[1],
        grad_key_query[:, key_width:],
        grad_key_query[:, :key_width] * key_scale,
        grad_value,
        grad_swish,
        grad_out,
        second_norm[0],
        second_norm[1],
        grad_gate,
        grad_up,
        grad_down,
    )


def solution(mesh):
    return jax.shard_map(
        shards,
        mesh=mesh,
        in_specs=(
            P(("sq", "head"), None),
            P("sq"),
            P("sq"),
            P("sq", "head"),
            P("sq", "head"),
            P("sq", "head"),
            P("sq", "head"),
            P("head", "sq"),
            P("sq"),
            P("sq"),
            P("sq", "head"),
            P("sq", "head"),
            P("head", "sq"),
            P(("sq", "head"), None),
        ),
        out_specs=(
            P(("sq", "head"), None),
            P(("sq", "head"), None),
            P(("head", "sq")),
            P(("head", "sq")),
            P("sq", "head"),
            P("sq", "head"),
            P("sq", "head"),
            P("sq", "head"),
            P("head", "sq"),
            P("sq"),
            P("sq"),
            P("sq", "head"),
            P("sq", "head"),
            P("head", "sq"),
        ),
        check_vma=False,
    )
```

profile of v0, /device:TPU:0, one launch (start us, length us, event | category | flops | bytes accessed | tf_op | source)
XLA Modules:
  0.0 750.4 jit_solution(14376096605201573835)
XLA Ops:
  33.3 4.2 collective-permute-done.refs_1_
  40.0 22.6 %collective-permute-done.8 = bf16[2,4,256]{2,1,0:T(4,128)(2,1)S(1)} collective-permute-done((bf16[2,4,256]{2,1,0:T(4,128)(2,1)S(1)}, bf16[2,4,256]{2,1,0:T(4,128)(2,1)S(1)}, u32[]{:S(2)}, u32[]{:S(2)}) %collective-permute-start.8) | collective-permute-done | bytes 4128 | tf_op jit(solution)/shard_map/ppermute | solution.py:33
  70.7 22.7 %collective-permute-done.13 = bf16[4,4,256]{2,1,0:T(4,128)(2,1)S(1)} collective-permute-done((bf16[4,4,256]{2,1,0:T(4,128)(2,1)S(1)}, bf16[4,4,256]{2,1,0:T(4,128)(2,1)S(1)}, u32[]{:S(2)}, u32[]{:S(2)}) %collective-permute-start.13) | collective-permute-done | bytes 8224 | tf_op jit(solution)/shard_map/ppermute | solution.py:33
  110.3 15.8 %shard_map.248 = (bf16[1024,2048]{1,0:T(8,128)(2,1)}, bf16[1024,2048]{1,0:T(8,128)(2,1)}, bf16[1024,1536]{1,0:T(8,128)(2,1)}, bf16[2048,2048]{1,0:T(8,128)(2,1)}) custom-call(s32[8]{0:T(128)S(1)} %stack.125.order, s32[4]{0:T(128)S(1)} %pad_add_fusion.1.start, bf16[256,2048]{1,0:T(8,128)(2,1)} %refs_0_, bf16[256,2048]{1,0:T(8,128)(2,1)} %collective-permute-done.refs_1_, ...), custom_call_target="tpu_custom_call" | custom-call | flops 1 | bytes 1 | tf_op jit(solution)/shard_map/pallas_call | solution.py:540
  150.6 10.9 %shard_map.250 = (bf16[1024,1536]{1,0:T(8,128)(2,1)S(1)}, bf16[2048,2048]{1,0:T(8,128)(2,1)S(1)}) custom-call(bf16[1024,2048]{1,0:T(8,128)(2,1)S(1)} %copy-done.10, bf16[256,2048]{1,0:T(8,128)(2,1)S(1)} %copy-done.33, bf16[256,2048]{1,0:T(8,128)(2,1)} %collective-permute-done.1.refs_0_.refs_6_.refs_1_, bf16[256,2048]{1,0:T(8,128)(2,1)S(1)} %copy-done.50, ...), custom_call_target="tpu_custom_call" | custom-call | flops 1 | bytes 1 | tf_op jit(solution)/shard_map/pallas_call | solution.py:576
  177.4 4.0 shard_map.252.first_ref
  182.7 4.9 shard_map.253
  192.6 5.1 shard_map.254
  205.6 8.1 %shard_map.256.whole_ref = bf16[768,2048]{1,0:T(8,128)(2,1)} custom-call(s32[3]{0:T(128)} %and_select_fusion.begin_ref, bf16[1024,1024]{1,0:T(8,128)(2,1)} %copy-done.4, bf16[1024,1024]{1,0:T(8,128)(2,1)} %copy-done.4, bf16[1024,1024]{1,0:T(8,128)(2,1)} %copy-done.4, bf16[1024,1024]{1,0:T(8,128)(2,1)} %copy-done.4, bf16[1024,1024]{1,0:T(8,128)(2,1)} %copy-done.4, ...), custom_call_target="tpu_custom_call" | custom-call | flops 1 | bytes 1 | tf_op jit(solution)/shard_map/pallas_call | solution.py:793
  216.1 14.4 %collective-permute-done.31.got_ref = bf16[256,2048]{1,0:T(8,128)(2,1)S(1)} collective-permute-done((bf16[256,2048]{1,0:T(8,128)(2,1)}, bf16[256,2048]{1,0:T(8,128)(2,1)S(1)}, u32[]{:S(2)}, u32[]{:S(2)}) %collective-permute-start.31) | collective-permute-done | bytes 1048608 | tf_op jit(solution)/shard_map/ppermute | solution.py:226
  234.2 25.3 %collective-permute-done.35.got_ref = bf16[256,2048]{1,0:T(8,128)(2,1)S(1)} collective-permute-done((bf16[256,2048]{1,0:T(8,128)(2,1)S(1)}, bf16[256,2048]{1,0:T(8,128)(2,1)S(1)}, u32[]{:S(2)}, u32[]{:S(2)}) %collective-permute-start.35) | collective-permute-done | bytes 1048608 | tf_op jit(solution)/shard_map/ppermute | solution.py:226
  263.1 23.8 %collective-permute-done.40.got_ref = bf16[256,2048]{1,0:T(8,128)(2,1)S(1)} collective-permute-done((bf16[256,2048]{1,0:T(8,128)(2,1)S(1)}, bf16[256,2048]{1,0:T(8,128)(2,1)S(1)}, u32[]{:S(2)}, u32[]{:S(2)}) %collective-permute-start.40) | collective-permute-done | bytes 1048608 | tf_op jit(solution)/shard_map/ppermute | solution.py:226
  291.9 9.5 %shard_map.264 = (bf16[256,1024]{1,0:T(8,128)(2,1)S(1)}, bf16[256,2048]{1,0:T(8,128)(2,1)S(1)}, f32[256,2048]{1,0:T(8,128)S(1)}, f32[256,2048]{1,0:T(8,128)S(1)}) custom-call(bf16[256,2048]{1,0:T(8,128)(2,1)S(1)} %add_convert_fusion.1.second_ref.refs_0_, bf16[256,2048]{1,0:T(8,128)(2,1)S(1)} %copy-done.16, bf16[256,1536]{1,0:T(8,128)(2,1)} %get-tuple-element.624.refs_0_, ...), custom_call_target="tpu_custom_call" | custom-call | flops 1 | bytes 1 | tf_op jit(solution)/shard_map/pallas_call | solution.py:676
  304.9 4.7 collective-permute-done.44.refs_0_.refs_14_.refs_3_
  310.0 5.2 collective-permute-done.43.second_ref.refs_1_
  320.8 21.1 %shard_map.266 = (bf16[256,1024]{1,0:T(8,128)(2,1)S(1)}, bf16[256,2048]{1,0:T(8,128)(2,1)}, bf16[256,1024]{1,0:T(8,128)(2,1)S(1)}, bf16[256,2048]{1,0:T(8,128)(2...) custom-call(bf16[256,2048]{1,0:T(8,128)(2,1)} %copy-done.28, ...), custom_call_target="tpu_custom_call" | custom-call | flops 1 | bytes 1 | tf_op jit(solution)/shard_map/pallas_call | solution.py:676
  344.5 4.8 shard_map.268
  352.4 10.7 %shard_map.267 = (bf16[256,1024]{1,0:T(8,128)(2,1)S(1)}, bf16[256,2048]{1,0:T(8,128)(2,1)S(1)}, f32[256,2048]{1,0:T(8,128)S(1)}, f32[256,2048]{1,0:T(8,128)S(1)}) custom-call(bf16[256,2048]{1,0:T(8,128)(2,1)S(1)} %add_convert_fusion.1.second_ref.refs_0_, bf16[256,2048]{1,0:T(8,128)(2,1)S(1)} %copy-done.16, ...), custom_call_target="tpu_custom_call" | custom-call | flops 1 | bytes 1 | tf_op jit(solution)/shard_map/pallas_call | solution.py:676
  366.8 4.7 shard_map.270
  371.6 5.4 shard_map.269
  384.7 6.0 shard_map.275
  390.7 5.9 shard_map.274
  396.6 6.7 shard_map.273
  411.6 6.3 shard_map.278
  417.8 16.6 %collective-permute-done.55.refs_1_ = bf16[512,1024]{1,0:T(8,128)(2,1)S(1)} collective-permute-done((bf16[512,1024]{1,0:T(8,128)(2,1)}, bf16[512,1024]{1,0:T(8,128)(2,1)S(1)}, u32[]{:S(2)}, u32[]{:S(2)}) %collective-permute-start.55) | collective-permute-done | bytes 1048608 | tf_op jit(solution)/shard_map/ppermute | solution.py:33
  437.2 7.2 shard_map.277
  453.1 6.1 shard_map.281
  460.7 21.3 %collective-permute-done.59.refs_1_ = bf16[256,1024]{1,0:T(8,128)(2,1)S(1)} collective-permute-done((bf16[256,1024]{1,0:T(8,128)(2,1)}, bf16[256,1024]{1,0:T(8,128)(2,1)S(1)}, u32[]{:S(2)}, u32[]{:S(2)}) %collective-permute-start.59) | collective-permute-done | bytes 524320 | tf_op jit(solution)/shard_map/ppermute | solution.py:33
  492.2 6.1 shard_map.282
  511.5 7.1 collective-permute-done.70.refs_1_
  523.4 4.5 shard_map.284
  529.1 13.7 %collective-permute-done.69 = bf16[256,1536]{1,0:T(8,128)(2,1)S(1)} collective-permute-done((bf16[256,1536]{1,0:T(8,128)(2,1)S(1)}, bf16[256,1536]{1,0:T(8,128)(2,1)S(1)}, u32[]{:S(2)}, u32[]{:S(2)}) %collective-permute-start.69) | collective-permute-done | bytes 786464 | tf_op jit(solution)/shard_map/ppermute | solution.py:271
  552.2 4.0 shard_map.286.last_ref
  561.0 6.1 shard_map.287.refs_0_.refs_2_.refs_3_.refs_5_.refs_6_.refs_8_.refs_1_
  569.1 9.1 %shard_map.288 = (bf16[256,2048]{1,0:T(8,128)(2,1)}, f32[2,2048]{1,0:T(2,128)}) custom-call(s32[1]{0:T(128)S(6)} %select_n.209.begin_ref, bf16[1024,2048]{1,0:T(8,128)(2,1)} %copy-done.1, bf16[1024,1024]{1,0:T(8,128)(2,1)} %get-tuple-element.789.refs_1_.refs_4_.refs_7_, bf16[1024,2048]{1,0:T(8,128)(2,1)} %copy-done.1, ...), custom_call_target="tpu_custom_call" | custom-call | flops 1 | bytes 1 | tf_op jit(solution)/shard_map/pallas_call | solution.py:793
  578.3 4.1 collective-permute-done.76
  584.6 7.2 shard_map.294
  591.8 5.9 shard_map.293
  601.3 17.4 %shard_map.290 = (bf16[768,2048]{1,0:T(8,128)(2,1)}, f32[2,2048]{1,0:T(2,128)}) custom-call(s32[3]{0:T(128)} %and_select_fusion.begin_ref, bf16[1024,2048]{1,0:T(8,128)(2,1)} %copy-done.1, bf16[1024,1024]{1,0:T(8,128)(2,1)} %get-tuple-element.789.refs_1_.refs_4_.refs_7_, bf16[1024,2048]{1,0:T(8,128)(2,1)} %copy-done.1, bf16[1024,2048]{1,0:T(8,128)(2,1)} %copy-done.1, ...), custom_call_target="tpu_custom_call" | custom-call | flops 1 | bytes 1 | tf_op jit(solution)/shard_map/pallas_call | solution.py:793
  627.9 8.9 %shard_map.295 = (bf16[512,1024]{1,0:T(8,128)(2,1)S(1)}, bf16[512,1024]{1,0:T(8,128)(2,1)}, bf16[512,1024]{1,0:T(8,128)(2,1)S(1)}, bf16[512,1024]{1,0:T(8,128)(2,1)}) custom-call(bf16[1024,2048]{1,0:T(8,128)(2,1)S(1)} %copy-done.13, bf16[1024,2048]{1,0:T(8,128)(2,1)S(1)} %copy-done.3, bf16[1024,2048]{1,0:T(8,128)(2,1)} %collective-permute-done.80.refs_2_), custom_call_target="tpu_custom_call" | custom-call | flops 1 | bytes 1 | tf_op jit(solution)/shard_map/pallas_call | solution.py:742
  636.9 4.4 shard_map.298
  654.6 14.6 %collective-permute-done.81.got_ref = bf16[256,2048]{1,0:T(8,128)(2,1)} collective-permute-done((bf16[256,2048]{1,0:T(8,128)(2,1)}, bf16[256,2048]{1,0:T(8,128)(2,1)}, u32[]{:S(2)}, u32[]{:S(2)}) %collective-permute-start.81) | collective-permute-done | bytes 1048608 | tf_op jit(solution)/shard_map/ppermute | solution.py:226
  675.6 4.9 shard_map.299
  689.0 12.0 %collective-permute-done.88.refs_1_ = bf16[256,512]{1,0:T(8,128)(2,1)S(1)} collective-permute-done((bf16[256,512]{1,0:T(8,128)(2,1)S(1)}, bf16[256,512]{1,0:T(8,128)(2,1)S(1)}, u32[]{:S(2)}, u32[]{:S(2)}) %collective-permute-start.88) | collective-permute-done | bytes 262176 | tf_op jit(solution)/shard_map/ppermute | solution.py:33
  702.8 4.7 collective-permute-done.85.got_ref
  719.6 4.0 collective-permute-start.97
  730.3 3.7 collective-permute-done.100.refs_1_
  736.8 9.7 %collective-permute-done.91 = bf16[256,2048]{1,0:T(8,128)(2,1)} collective-permute-done((bf16[256,2048]{1,0:T(8,128)(2,1)}, bf16[256,2048]{1,0:T(8,128)(2,1)}, u32[]{:S(2)}, u32[]{:S(2)}) %collective-permute-start.91) | collective-permute-done | bytes 1048608 | tf_op jit(solution)/shard_map/ppermute | solution.py:271
  (737 shorter events, 290.8 us)
Async XLA Ops:
  3.7 29.5 %collective-permute-start.1 = (bf16[256,2048]{1,0:T(8,128)(2,1)S(1)}, bf16[256,2048]{1,0:T(8,128)(2,1)}, u32[]{:S(2)}, u32[]{:S(2)}) collective-permute-start(bf16[256,2048]{1,0:T(8,128)(2,1)S(1)} %get-tuple-element.502.refs_0_.refs_5_), channel_id=1, source_target_pairs={{0,2},{1,3},{2,0},{3,1},{4,6},{5,7},{6,4},{7,5},{8,10},{9,11},{10,... | collective-permute-start | bytes 3145736 | tf_op jit(solution)/shard_map/ppermute | solution.py:33
  9.7 27.8 %collective-permute-start.3 = (bf16[2,256,2048]{2,1,0:T(8,128)(2,1)}, bf16[2,256,2048]{2,1,0:T(8,128)(2,1)}, u32[]{:S(2)}, u32[]{:S(2)}) collective-permute-start(bf16[2,256,2048]{2,1,0:T(8,128)(2,1)} %shard_map.245), channel_id=1, source_target_pairs={{0,1},{1,0},{2,3},{3,2},{4,5},{5,4},{6,7},{7,6},{8,9},{9,8},{10,11... | collective-permute-start | bytes 6291464 | tf_op jit(solution)/shard_map/ppermute | solution.py:33
  9.7 27.7 %collective-permute-start = (bf16[256,2048]{1,0:T(8,128)(2,1)}, bf16[256,2048]{1,0:T(8,128)(2,1)}, u32[]{:S(2)}, u32[]{:S(2)}) collective-permute-start(bf16[256,2048]{1,0:T(8,128)(2,1)} %refs_0_), channel_id=1, source_target_pairs={{0,8},{8,16},{16,24},{24,0},{1,9},{9,17},{17,25},{25,1},{2,10},{10... | collective-permute-start | bytes 3145736 | tf_op jit(solution)/shard_map/ppermute | solution.py:226
  37.5 26.9 %collective-permute-start.5 = (bf16[256,2048]{1,0:T(8,128)(2,1)}, bf16[256,2048]{1,0:T(8,128)(2,1)S(1)}, u32[]{:S(2)}, u32[]{:S(2)}) collective-permute-start(bf16[256,2048]{1,0:T(8,128)(2,1)} %collective-permute-done.refs_1_), channel_id=1, source_target_pairs={{0,8},{8,16},{16,24},{24,0},{1,9},{9,17},{17,25},{25,1},{2,10},{10... | collective-permute-start | bytes 3145736 | tf_op jit(solution)/shard_map/ppermute | solution.py:226
  37.5 26.9 %collective-permute-start.6 = (bf16[256,2048]{1,0:T(8,128)(2,1)S(1)}, bf16[256,2048]{1,0:T(8,128)(2,1)S(1)}, u32[]{:S(2)}, u32[]{:S(2)}) collective-permute-start(bf16[256,2048]{1,0:T(8,128)(2,1)S(1)} %get-tuple-element.502.refs_0_.refs_5_), channel_id=1, source_target_pairs={{0,4},{1,5},{2,6},{3,7},{4,0},{5,1},{6,2},{7,3},{8,12},{9,13},{10,... | collective-permute-start | bytes 3145736 | tf_op jit(solution)/shard_map/ppermute | solution.py:33
  67.3 29.5 %collective-permute-start.12 = (bf16[4,256,2048]{2,1,0:T(8,128)(2,1)S(1)}, bf16[4,256,2048]{2,1,0:T(8,128)(2,1)}, u32[]{:S(2)}, u32[]{:S(2)}) collective-permute-start(bf16[4,256,2048]{2,1,0:T(8,128)(2,1)S(1)} %shard_map.246), channel_id=1, source_target_pairs={{0,1},{1,0},{2,3},{3,2},{4,5},{5,4},{6,7},{7,6},{8,9},{9,8},{10,11... | collective-permute-start | bytes 12582920 | tf_op jit(solution)/shard_map/ppermute | solution.py:33
  68.7 27.2 %collective-permute-start.9 = (bf16[256,2048]{1,0:T(8,128)(2,1)S(1)}, bf16[256,2048]{1,0:T(8,128)(2,1)S(1)}, u32[]{:S(2)}, u32[]{:S(2)}) collective-permute-start(bf16[256,2048]{1,0:T(8,128)(2,1)S(1)} %collective-permute-done.5.refs_2_), channel_id=1, source_target_pairs={{0,8},{8,16},{16,24},{24,0},{1,9},{9,17},{17,25},{25,1},{2,10},{10... | collective-permute-start | bytes 3145736 | tf_op jit(solution)/shard_map/ppermute | solution.py:226
  98.4 37.0 %collective-permute-start.16 = (bf16[256,2048]{1,0:T(8,128)(2,1)S(1)}, bf16[256,2048]{1,0:T(8,128)(2,1)}, u32[]{:S(2)}, u32[]{:S(2)}) collective-permute-start(bf16[256,2048]{1,0:T(8,128)(2,1)S(1)} %dynamic-slice_dynamic-update-slice_fusion.24.cot_ref.refs_0_), channel_id=1, source_target_pairs={{0,8},{8,0},{16,24},{24,16},{1,9},{9,1},{17,25},{25,17},{2,10},{10... | collective-permute-start | bytes 3145736 | tf_op jit(solution)/shard_map/ppermute | solution.py:271
  101.1 32.0 %collective-permute-start.17 = (bf16[256,1536]{1,0:T(8,128)(2,1)}, bf16[256,1536]{1,0:T(8,128)(2,1)S(1)}, u32[]{:S(2)}, u32[]{:S(2)}) collective-permute-start(bf16[256,1536]{1,0:T(8,128)(2,1)} %get-tuple-element.624.refs_0_), channel_id=1, source_target_pairs={{0,2},{1,3},{2,0},{3,1},{4,6},{5,7},{6,4},{7,5},{8,10},{9,11},{10,... | collective-permute-start | bytes 2359304 | tf_op jit(solution)/shard_map/ppermute | solution.py:33
  103.5 30.5 %collective-permute-start.18 = (bf16[256,1536]{1,0:T(8,128)(2,1)}, bf16[256,1536]{1,0:T(8,128)(2,1)S(1)}, u32[]{:S(2)}, u32[]{:S(2)}) collective-permute-start(bf16[256,1536]{1,0:T(8,128)(2,1)} %get-tuple-element.628.refs_1_.refs_4_), channel_id=1, source_target_pairs={{0,4},{1,5},{2,6},{3,7},{4,0},{5,1},{6,2},{7,3},{8,12},{9,13},{10,... | collective-permute-start | bytes 2359304 | tf_op jit(solution)/shard_map/ppermute | solution.py:33
  106.2 26.9 %collective-permute-start.15 = (bf16[256,1024]{1,0:T(8,128)(2,1)S(1)}, bf16[256,1024]{1,0:T(8,128)(2,1)S(1)}, u32[]{:S(2)}, u32[]{:S(2)}) collective-permute-start(bf16[256,1024]{1,0:T(8,128)(2,1)S(1)} %slice.109), channel_id=1, source_target_pairs={{0,16},{8,24},{16,0},{24,8},{1,17},{9,25},{17,1},{25,9},{2,18},{10... | collective-permute-start | bytes 1572872 | tf_op jit(solution)/shard_map/ppermute | solution.py:271
  138.2 26.6 %collective-permute-start.25 = (bf16[256,1024]{1,0:T(8,128)(2,1)S(1)}, bf16[256,1024]{1,0:T(8,128)(2,1)S(1)}, u32[]{:S(2)}, u32[]{:S(2)}) collective-permute-start(bf16[256,1024]{1,0:T(8,128)(2,1)S(1)} %slice.110), channel_id=1, source_target_pairs={{0,16},{8,24},{16,0},{24,8},{1,17},{9,25},{17,1},{25,9},{2,18},{10... | collective-permute-start | bytes 1572872 | tf_op jit(solution)/shard_map/ppermute | solution.py:271
  171.0 28.7 %collective-permute-start.29 = (bf16[2,256,1536]{2,1,0:T(8,128)(2,1)}, bf16[2,256,1536]{2,1,0:T(8,128)(2,1)}, u32[]{:S(2)}, u32[]{:S(2)}) collective-permute-start(bf16[2,256,1536]{2,1,0:T(8,128)(2,1)} %shard_map.255), channel_id=1, source_target_pairs={{0,1},{1,0},{2,3},{3,2},{4,5},{5,4},{6,7},{7,6},{8,9},{9,8},{10,11... | collective-permute-start | bytes 4718600 | tf_op jit(solution)/shard_map/ppermute | solution.py:33
  171.5 28.1 %collective-permute-start.27 = (bf16[256,1536]{1,0:T(8,128)(2,1)}, bf16[256,1536]{1,0:T(8,128)(2,1)}, u32[]{:S(2)}, u32[]{:S(2)}) collective-permute-start(bf16[256,1536]{1,0:T(8,128)(2,1)} %get-tuple-element.624.refs_0_), channel_id=1, source_target_pairs={{0,4},{1,5},{2,6},{3,7},{4,0},{5,1},{6,2},{7,3},{8,12},{9,13},{10,... | collective-permute-start | bytes 2359304 | tf_op jit(solution)/shard_map/ppermute | solution.py:33
  173.0 26.6 %collective-permute-start.28 = (bf16[256,1536]{1,0:T(8,128)(2,1)}, bf16[256,1536]{1,0:T(8,128)(2,1)}, u32[]{:S(2)}, u32[]{:S(2)}) collective-permute-start(bf16[256,1536]{1,0:T(8,128)(2,1)} %get-tuple-element.628.refs_1_.refs_4_), channel_id=1, source_target_pairs={{0,2},{1,3},{2,0},{3,1},{4,6},{5,7},{6,4},{7,5},{8,10},{9,11},{10,... | collective-permute-start | bytes 2359304 | tf_op jit(solution)/shard_map/ppermute | solution.py:33
  202.9 28.1 %collective-permute-start.34 = (bf16[4,256,1536]{2,1,0:T(8,128)(2,1)}, bf16[4,256,1536]{2,1,0:T(8,128)(2,1)S(1)}, u32[]{:S(2)}, u32[]{:S(2)}) collective-permute-start(bf16[4,256,1536]{2,1,0:T(8,128)(2,1)} %shard_map.258), channel_id=1, source_target_pairs={{0,1},{1,0},{2,3},{3,2},{4,5},{5,4},{6,7},{7,6},{8,9},{9,8},{10,11... | collective-permute-start | bytes 9437192 | tf_op jit(solution)/shard_map/ppermute | solution.py:33
  202.9 27.6 %collective-permute-start.31 = (bf16[256,2048]{1,0:T(8,128)(2,1)}, bf16[256,2048]{1,0:T(8,128)(2,1)S(1)}, u32[]{:S(2)}, u32[]{:S(2)}) collective-permute-start(bf16[256,2048]{1,0:T(8,128)(2,1)} %shard_map.254), channel_id=1, source_target_pairs={{0,8},{8,16},{16,24},{24,0},{1,9},{9,17},{17,25},{25,1},{2,10},{10... | collective-permute-start | bytes 3145736 | tf_op jit(solution)/shard_map/ppermute | solution.py:226
  202.9 28.1 %collective-permute-start.32 = (bf16[256,1536]{1,0:T(8,128)(2,1)S(1)}, bf16[256,1536]{1,0:T(8,128)(2,1)S(1)}, u32[]{:S(2)}, u32[]{:S(2)}) collective-permute-start(bf16[256,1536]{1,0:T(8,128)(2,1)S(1)} %copy-done.54), channel_id=1, source_target_pairs={{0,4},{1,5},{2,6},{3,7},{4,0},{5,1},{6,2},{7,3},{8,12},{9,13},{10,... | collective-permute-start | bytes 2359304 | tf_op jit(solution)/shard_map/ppermute | solution.py:33
  203.6 27.4 %collective-permute-start.33 = (bf16[256,1536]{1,0:T(8,128)(2,1)S(1)}, bf16[256,1536]{1,0:T(8,128)(2,1)S(1)}, u32[]{:S(2)}, u32[]{:S(2)}) collective-permute-start(bf16[256,1536]{1,0:T(8,128)(2,1)S(1)} %copy-done.56), channel_id=1, source_target_pairs={{0,2},{1,3},{2,0},{3,1},{4,6},{5,7},{6,4},{7,5},{8,10},{9,11},{10,... | collective-permute-start | bytes 2359304 | tf_op jit(solution)/shard_map/ppermute | solution.py:33
  231.2 28.9 %collective-permute-start.39 = (bf16[2,256,1536]{2,1,0:T(8,128)(2,1)S(1)}, bf16[2,256,1536]{2,1,0:T(8,128)(2,1)S(1)}, u32[]{:S(2)}, u32[]{:S(2)}) collective-permute-start(bf16[2,256,1536]{2,1,0:T(8,128)(2,1)S(1)} %shard_map.261), channel_id=1, source_target_pairs={{0,1},{1,0},{2,3},{3,2},{4,5},{5,4},{6,7},{7,6},{8,9},{9,8},{10,11... | collective-permute-start | bytes 4718600 | tf_op jit(solution)/shard_map/ppermute | solution.py:33
  232.1 27.9 %collective-permute-start.36 = (bf16[2,256,1536]{2,1,0:T(8,128)(2,1)S(1)}, bf16[2,256,1536]{2,1,0:T(8,128)(2,1)S(1)}, u32[]{:S(2)}, u32[]{:S(2)}) collective-permute-start(bf16[2,256,1536]{2,1,0:T(8,128)(2,1)S(1)} %shard_map.260), channel_id=1, source_target_pairs={{0,1},{1,0},{2,3},{3,2},{4,5},{5,4},{6,7},{7,6},{8,9},{9,8},{10,11... | collective-permute-start | bytes 4718600 | tf_op jit(solution)/shard_map/ppermute | solution.py:33
  232.1 27.4 %collective-permute-start.35 = (bf16[256,2048]{1,0:T(8,128)(2,1)S(1)}, bf16[256,2048]{1,0:T(8,128)(2,1)S(1)}, u32[]{:S(2)}, u32[]{:S(2)}) collective-permute-start(bf16[256,2048]{1,0:T(8,128)(2,1)S(1)} %shard_map.257), channel_id=1, source_target_pairs={{0,8},{8,16},{16,24},{24,0},{1,9},{9,17},{17,25},{25,1},{2,10},{10... | collective-permute-start | bytes 3145736 | tf_op jit(solution)/shard_map/ppermute | solution.py:226
  232.1 27.9 %collective-permute-start.37 = (bf16[256,1536]{1,0:T(8,128)(2,1)S(1)}, bf16[256,1536]{1,0:T(8,128)(2,1)S(1)}, u32[]{:S(2)}, u32[]{:S(2)}) collective-permute-start(bf16[256,1536]{1,0:T(8,128)(2,1)S(1)} %pad_maximum_fusion.5.refs_0_.refs_11_), channel_id=1, source_target_pairs={{0,2},{1,3},{2,0},{3,1},{4,6},{5,7},{6,4},{7,5},{8,10},{9,11},{10,... | collective-permute-start | bytes 2359304 | tf_op jit(solution)/shard_map/ppermute | solution.py:33
  260.1 26.8 %collective-permute-start.40 = (bf16[256,2048]{1,0:T(8,128)(2,1)S(1)}, bf16[256,2048]{1,0:T(8,128)(2,1)S(1)}, u32[]{:S(2)}, u32[]{:S(2)}) collective-permute-start(bf16[256,2048]{1,0:T(8,128)(2,1)S(1)} %shard_map.259), channel_id=1, source_target_pairs={{0,8},{8,16},{16,24},{24,0},{1,9},{9,17},{17,25},{25,1},{2,10},{10... | collective-permute-start | bytes 3145736 | tf_op jit(solution)/shard_map/ppermute | solution.py:226
  260.3 27.1 %collective-permute-start.41 = (bf16[256,1536]{1,0:T(8,128)(2,1)S(1)}, bf16[256,1536]{1,0:T(8,128)(2,1)S(1)}, u32[]{:S(2)}, u32[]{:S(2)}) collective-permute-start(bf16[256,1536]{1,0:T(8,128)(2,1)S(1)} %pad_maximum_fusion.5.refs_0_.refs_11_), channel_id=1, source_target_pairs={{0,4},{1,5},{2,6},{3,7},{4,0},{5,1},{6,2},{7,3},{8,12},{9,13},{10,... | collective-permute-start | bytes 2359304 | tf_op jit(solution)/shard_map/ppermute | solution.py:33
  349.5 27.6 %collective-permute-start.48 = (bf16[256,2048]{1,0:T(8,128)(2,1)S(1)}, bf16[256,2048]{1,0:T(8,128)(2,1)S(1)}, u32[]{:S(2)}, u32[]{:S(2)}) collective-permute-start(bf16[256,2048]{1,0:T(8,128)(2,1)S(1)} %copy-done.187), channel_id=1, source_target_pairs={{0,8},{8,0},{16,24},{24,16},{1,9},{9,1},{17,25},{25,17},{2,10},{10... | collective-permute-start | bytes 3145736 | tf_op jit(solution)/shard_map/ppermute | solution.py:271
  380.9 27.6 %collective-permute-start.50 = (bf16[256,2048]{1,0:T(8,128)(2,1)}, bf16[256,2048]{1,0:T(8,128)(2,1)}, u32[]{:S(2)}, u32[]{:S(2)}) collective-permute-start(bf16[256,2048]{1,0:T(8,128)(2,1)} %fusion.5.branch_ref), channel_id=1, source_target_pairs={{0,8},{8,16},{16,24},{24,0},{1,9},{9,17},{17,25},{25,1},{2,10},{10... | collective-permute-start | bytes 3145736 | tf_op jit(solution)/shard_map/ppermute | solution.py:226
  408.6 28.6 %collective-permute-start.57 = (bf16[1024,2048]{1,0:T(8,128)(2,1)}, bf16[1024,2048]{1,0:T(8,128)(2,1)}, u32[]{:S(2)}, u32[]{:S(2)}) collective-permute-start(bf16[1024,2048]{1,0:T(8,128)(2,1)} %shard_map.274), channel_id=1, source_target_pairs={{0,1},{1,0},{2,3},{3,2},{4,5},{5,4},{6,7},{7,6},{8,9},{9,8},{10,11... | collective-permute-start | bytes 12582920 | tf_op jit(solution)/shard_map/ppermute | solution.py:33
  411.3 34.2 %collective-permute-start.54 = (bf16[256,2048]{1,0:T(8,128)(2,1)}, bf16[256,2048]{1,0:T(8,128)(2,1)}, u32[]{:S(2)}, u32[]{:S(2)}) collective-permute-start(bf16[256,2048]{1,0:T(8,128)(2,1)} %collective-permute-done.50.branch_ref), channel_id=1, source_target_pairs={{0,8},{8,16},{16,24},{24,0},{1,9},{9,17},{17,25},{25,1},{2,10},{10... | collective-permute-start | bytes 3145736 | tf_op jit(solution)/shard_map/ppermute | solution.py:226
  445.5 40.3 %collective-permute-start.61 = (bf16[512,1024]{1,0:T(8,128)(2,1)}, bf16[512,1024]{1,0:T(8,128)(2,1)}, u32[]{:S(2)}, u32[]{:S(2)}) collective-permute-start(bf16[512,1024]{1,0:T(8,128)(2,1)} %get-tuple-element.734), channel_id=1, source_target_pairs={{0,4},{1,5},{2,6},{3,7},{4,0},{5,1},{6,2},{7,3},{8,12},{9,13},{10,... | collective-permute-start | bytes 3145736 | tf_op jit(solution)/shard_map/ppermute | solution.py:33
  446.3 39.5 %collective-permute-start.62 = (bf16[512,1024]{1,0:T(8,128)(2,1)}, bf16[512,1024]{1,0:T(8,128)(2,1)}, u32[]{:S(2)}, u32[]{:S(2)}) collective-permute-start(bf16[512,1024]{1,0:T(8,128)(2,1)} %get-tuple-element.736), channel_id=1, source_target_pairs={{0,2},{1,3},{2,0},{3,1},{4,6},{5,7},{6,4},{7,5},{8,10},{9,11},{10,... | collective-permute-start | bytes 3145736 | tf_op jit(solution)/shard_map/ppermute | solution.py:33
  447.6 40.2 %collective-permute-start.58 = (bf16[256,2048]{1,0:T(8,128)(2,1)}, bf16[256,2048]{1,0:T(8,128)(2,1)}, u32[]{:S(2)}, u32[]{:S(2)}) collective-permute-start(bf16[256,2048]{1,0:T(8,128)(2,1)} %collective-permute-done.54.branch_ref), channel_id=1, source_target_pairs={{0,8},{8,16},{16,24},{24,0},{1,9},{9,17},{17,25},{25,1},{2,10},{10... | collective-permute-start | bytes 3145736 | tf_op jit(solution)/shard_map/ppermute | solution.py:226
  447.9 34.1 %collective-permute-start.59 = (bf16[256,1024]{1,0:T(8,128)(2,1)}, bf16[256,1024]{1,0:T(8,128)(2,1)S(1)}, u32[]{:S(2)}, u32[]{:S(2)}) collective-permute-start(bf16[256,1024]{1,0:T(8,128)(2,1)} %copy-done.159), channel_id=1, source_target_pairs={{0,2},{1,3},{2,0},{3,1},{4,6},{5,7},{6,4},{7,5},{8,10},{9,11},{10,... | collective-permute-start | bytes 1572872 | tf_op jit(solution)/shard_map/ppermute | solution.py:33
  448.6 33.4 %collective-permute-start.60 = (bf16[256,1024]{1,0:T(8,128)(2,1)}, bf16[256,1024]{1,0:T(8,128)(2,1)S(1)}, u32[]{:S(2)}, u32[]{:S(2)}) collective-permute-start(bf16[256,1024]{1,0:T(8,128)(2,1)} %copy-done.158), channel_id=1, source_target_pairs={{0,4},{1,5},{2,6},{3,7},{4,0},{5,1},{6,2},{7,3},{8,12},{9,13},{10,... | collective-permute-start | bytes 1572872 | tf_op jit(solution)/shard_map/ppermute | solution.py:33
  509.3 33.6 %collective-permute-start.69 = (bf16[256,1536]{1,0:T(8,128)(2,1)S(1)}, bf16[256,1536]{1,0:T(8,128)(2,1)S(1)}, u32[]{:S(2)}, u32[]{:S(2)}) collective-permute-start(bf16[256,1536]{1,0:T(8,128)(2,1)S(1)} %pad_maximum_fusion.7), channel_id=1, source_target_pairs={{0,16},{8,24},{16,0},{24,8},{1,17},{9,25},{17,1},{25,9},{2,18},{10... | collective-permute-start | bytes 2359304 | tf_op jit(solution)/shard_map/ppermute | solution.py:271
  544.5 37.9 %collective-permute-start.75 = (bf16[1024,1024]{1,0:T(8,128)(2,1)}, bf16[1024,1024]{1,0:T(8,128)(2,1)}, u32[]{:S(2)}, u32[]{:S(2)}) collective-permute-start(bf16[1024,1024]{1,0:T(8,128)(2,1)} %shard_map.284), channel_id=1, source_target_pairs={{0,1},{1,0},{2,3},{3,2},{4,5},{5,4},{6,7},{7,6},{8,9},{9,8},{10,11... | collective-permute-start | bytes 6291464 | tf_op jit(solution)/shard_map/ppermute | solution.py:33
  546.0 36.4 %collective-permute-start.76 = (bf16[256,1536]{1,0:T(8,128)(2,1)}, bf16[256,1536]{1,0:T(8,128)(2,1)}, u32[]{:S(2)}, u32[]{:S(2)}) collective-permute-start(bf16[256,1536]{1,0:T(8,128)(2,1)} %pad_maximum_fusion.8), channel_id=1, source_target_pairs={{0,16},{8,24},{16,0},{24,8},{1,17},{9,25},{17,1},{25,9},{2,18},{10... | collective-permute-start | bytes 2359304 | tf_op jit(solution)/shard_map/ppermute | solution.py:271
  549.4 28.8 %collective-permute-start.73 = (bf16[256,1024]{1,0:T(8,128)(2,1)}, bf16[256,1024]{1,0:T(8,128)(2,1)}, u32[]{:S(2)}, u32[]{:S(2)}) collective-permute-start(bf16[256,1024]{1,0:T(8,128)(2,1)} %get-tuple-element.805), channel_id=1, source_target_pairs={{0,2},{1,3},{2,0},{3,1},{4,6},{5,7},{6,4},{7,5},{8,10},{9,11},{10,... | collective-permute-start | bytes 1572872 | tf_op jit(solution)/shard_map/ppermute | solution.py:33
  550.8 27.5 %collective-permute-start.74 = (bf16[256,1024]{1,0:T(8,128)(2,1)}, bf16[256,1024]{1,0:T(8,128)(2,1)}, u32[]{:S(2)}, u32[]{:S(2)}) collective-permute-start(bf16[256,1024]{1,0:T(8,128)(2,1)} %get-tuple-element.807), channel_id=1, source_target_pairs={{0,4},{1,5},{2,6},{3,7},{4,0},{5,1},{6,2},{7,3},{8,12},{9,13},{10,... | collective-permute-start | bytes 1572872 | tf_op jit(solution)/shard_map/ppermute | solution.py:33
  591.8 35.6 %collective-permute-start.80 = (bf16[1024,2048]{1,0:T(8,128)(2,1)}, bf16[1024,2048]{1,0:T(8,128)(2,1)}, u32[]{:S(2)}, u32[]{:S(2)}) collective-permute-start(bf16[1024,2048]{1,0:T(8,128)(2,1)} %shard_map.294), channel_id=1, source_target_pairs={{0,1},{1,0},{2,3},{3,2},{4,5},{5,4},{6,7},{7,6},{8,9},{9,8},{10,11... | collective-permute-start | bytes 12582920 | tf_op jit(solution)/shard_map/ppermute | solution.py:33
  591.8 31.4 %collective-permute-start.77 = (bf16[256,2048]{1,0:T(8,128)(2,1)}, bf16[256,2048]{1,0:T(8,128)(2,1)}, u32[]{:S(2)}, u32[]{:S(2)}) collective-permute-start(bf16[256,2048]{1,0:T(8,128)(2,1)} %get-tuple-element.817), channel_id=1, source_target_pairs={{0,8},{8,16},{16,24},{24,0},{1,9},{9,17},{17,25},{25,1},{2,10},{10... | collective-permute-start | bytes 3145736 | tf_op jit(solution)/shard_map/ppermute | solution.py:226
  599.3 37.6 %collective-permute-start.78 = (bf16[512,512]{1,0:T(8,128)(2,1)}, bf16[512,512]{1,0:T(8,128)(2,1)}, u32[]{:S(2)}, u32[]{:S(2)}) collective-permute-start(bf16[512,512]{1,0:T(8,128)(2,1)} %get-tuple-element.826), channel_id=1, source_target_pairs={{0,4},{1,5},{2,6},{3,7},{4,0},{5,1},{6,2},{7,3},{8,12},{9,13},{10,... | collective-permute-start | bytes 1572872 | tf_op jit(solution)/shard_map/ppermute | solution.py:33
  600.0 36.9 %collective-permute-start.79 = (bf16[512,512]{1,0:T(8,128)(2,1)}, bf16[512,512]{1,0:T(8,128)(2,1)}, u32[]{:S(2)}, u32[]{:S(2)}) collective-permute-start(bf16[512,512]{1,0:T(8,128)(2,1)} %get-tuple-element.828), channel_id=1, source_target_pairs={{0,2},{1,3},{2,0},{3,1},{4,6},{5,7},{6,4},{7,5},{8,10},{9,11},{10,... | collective-permute-start | bytes 1572872 | tf_op jit(solution)/shard_map/ppermute | solution.py:33
  641.3 33.8 %collective-permute-start.84 = (bf16[1024,1024]{1,0:T(8,128)(2,1)}, bf16[1024,1024]{1,0:T(8,128)(2,1)}, u32[]{:S(2)}, u32[]{:S(2)}) collective-permute-start(bf16[1024,1024]{1,0:T(8,128)(2,1)} %shard_map.298), channel_id=1, source_target_pairs={{0,1},{1,0},{2,3},{3,2},{4,5},{5,4},{6,7},{7,6},{8,9},{9,8},{10,11... | collective-permute-start | bytes 6291464 | tf_op jit(solution)/shard_map/ppermute | solution.py:33
  641.3 27.9 %collective-permute-start.81 = (bf16[256,2048]{1,0:T(8,128)(2,1)}, bf16[256,2048]{1,0:T(8,128)(2,1)}, u32[]{:S(2)}, u32[]{:S(2)}) collective-permute-start(bf16[256,2048]{1,0:T(8,128)(2,1)} %shard_map.291), channel_id=1, source_target_pairs={{0,8},{8,16},{16,24},{24,0},{1,9},{9,17},{17,25},{25,1},{2,10},{10... | collective-permute-start | bytes 3145736 | tf_op jit(solution)/shard_map/ppermute | solution.py:226
  641.5 31.3 %collective-permute-start.82 = (bf16[512,1024]{1,0:T(8,128)(2,1)}, bf16[512,1024]{1,0:T(8,128)(2,1)}, u32[]{:S(2)}, u32[]{:S(2)}) collective-permute-start(bf16[512,1024]{1,0:T(8,128)(2,1)} %get-tuple-element.844), channel_id=1, source_target_pairs={{0,4},{1,5},{2,6},{3,7},{4,0},{5,1},{6,2},{7,3},{8,12},{9,13},{10,... | collective-permute-start | bytes 3145736 | tf_op jit(solution)/shard_map/ppermute | solution.py:33
  642.8 30.0 %collective-permute-start.83 = (bf16[512,1024]{1,0:T(8,128)(2,1)}, bf16[512,1024]{1,0:T(8,128)(2,1)}, u32[]{:S(2)}, u32[]{:S(2)}) collective-permute-start(bf16[512,1024]{1,0:T(8,128)(2,1)} %get-tuple-element.846), channel_id=1, source_target_pairs={{0,2},{1,3},{2,0},{3,1},{4,6},{5,7},{6,4},{7,5},{8,10},{9,11},{10,... | collective-permute-start | bytes 3145736 | tf_op jit(solution)/shard_map/ppermute | solution.py:33
  680.5 27.0 %collective-permute-start.85 = (bf16[256,2048]{1,0:T(8,128)(2,1)S(1)}, bf16[256,2048]{1,0:T(8,128)(2,1)S(1)}, u32[]{:S(2)}, u32[]{:S(2)}) collective-permute-start(bf16[256,2048]{1,0:T(8,128)(2,1)S(1)} %shard_map.296), channel_id=1, source_target_pairs={{0,8},{8,16},{16,24},{24,0},{1,9},{9,17},{17,25},{25,1},{2,10},{10... | collective-permute-start | bytes 3145736 | tf_op jit(solution)/shard_map/ppermute | solution.py:226
  (246 other events, 2736.2 us)
where the time goes:
time: 755 us; the launch traced here: 750 us
  waiting for transfers between devices  264 us (35%)
  Pallas kernels  259 us (34%)
  local copies, waits for them, and re-layouts  112 us (15%)
  starting transfers between devices  84.4 us (11%)
  other arithmetic  27.7 us (4%)
    ppermute x74, waiting for transfers between devices, flip(): return lax.ppermute(value, 'sq', [(i, i ^ mask) for i in range(count)])  128 us
    ppermute x12, waiting for transfers between devices, ring_step(): lax.ppermute(value, 'head', [(i, (i + 1) % count) for i in range(count)])  94.3 us
    unnamed x429, local copies, waits for them, and re-layouts  90.3 us
    pallas_call x12, Pallas kernels, outer_half(): call(functools.partial(outer_kernel, len(lefts), len(extra), rows, bits),...  70.6 us
    ppermute x74, starting transfers between devices, flip(): return lax.ppermute(value, 'sq', [(i, i ^ mask) for i in range(count)])  63.9 us
    pallas_call x3, Pallas kernels, feed_part(): pl.pallas_call(functools.partial(feed_kernel, top, quarter, places, sizes...  41.3 us
    pallas_call x4, Pallas kernels, rows_back(): pl.pallas_call(functools.partial(rows_kernel, parts, sides, int(xhat is n...  39.7 us
    ppermute x9, waiting for transfers between devices, swap_head(): return lax.ppermute(value, 'head', [(i, i ^ mask) for i in range(count)])  38.1 us
  transfers between devices with their start and end apart: 102, of which 38 were waited for; matrix products, arithmetic and copies ran while one was open for 8% of the time, Pallas kernels for 26%

commit v1 on v0

--- a/solution.py
+++ b/solution.py
@@ -110,6 +110,16 @@
     def rest(self):
         self.send(len(self.todo[0]))
 
+    def rest_grouped(self):
+        for k, held in enumerate(self.pieces):
+            while self.todo[k]:
+                bit = self.todo[k][0][1]
+                slots = [s for s, b in self.todo[k] if b == bit]
+                self.todo[k] = self.todo[k][len(slots) :]
+                got = flip(stack([held[s] for s in slots]), mask_of(1 << bit, self.count))
+                for i, slot in enumerate(slots):
+                    held[slot | 1 << bit] = got[i]
+
     def core(self):
         sent = [s for slots, _ in self.far for s in slots]
         ready = [s for s in range(self.top) if s not in sent and all(s in h for h in self.pieces)]
@@ -212,6 +222,26 @@
         self.held = list(values)
 
 
+def send_together(*sums):
+    wanted = {}
+    for thing in sums:
+        thing.merge()
+        for k in range(2):
+            wanted.setdefault(thing.todo[k][0], []).append((thing, k))
+    for bit, group in wanted.items():
+        parts = [thing.held[2 * k + 1] for thing, k in group]
+        got = flip(above(parts) if len(parts) > 1 else parts[0], mask_of(1 << bit, sums[0].count))
+        begin = 0
+        for (thing, k), part in zip(group, parts):
+            thing.held[2 * k + 1] = got[begin : begin + part.shape[0]]
+            begin += part.shape[0]
+            thing.todo[k] = thing.todo[k][1:]
+            thing.slots[k] = [s for s in thing.slots[k] if not s >> bit & 1]
+    for thing in sums:
+        thing.arrived = True
+        thing.merge()
+
+
 def settle(*things):
     values = lax.optimization_barrier(tuple(v for t in things for v in t.get()))
     values = list(values)
@@ -303,6 +333,26 @@
         in_specs=[vmem] * len(pieces),
         out_specs=vmem,
         out_shape=jax.ShapeDtypeStruct((pieces[0].shape[0], columns), pieces[0].dtype),
+        compiler_params=pltpu.CompilerParams(vmem_limit_bytes=16 * 2**20),
+        cost_estimate=brief,
+    )(*pieces)
+
+
+def above_kernel(*refs):
+    begin = 0
+    for ref in refs[:-1]:
+        refs[-1][pl.ds(begin, ref.shape[0]), :] = ref[...]
+        begin += ref.shape[0]
+
+
+def above(pieces):
+    vmem = pl.BlockSpec(memory_space=pltpu.VMEM)
+    rows = sum(p.shape[0] for p in pieces)
+    return pl.pallas_call(
+        above_kernel,
+        in_specs=[vmem] * len(pieces),
+        out_specs=vmem,
+        out_shape=jax.ShapeDtypeStruct((rows, pieces[0].shape[1]), pieces[0].dtype),
         compiler_params=pltpu.CompilerParams(vmem_limit_bytes=16 * 2**20),
         cost_estimate=brief,
     )(*pieces)
@@ -1084,6 +1134,11 @@
     down_shard = w_down.T
     feed_first = Box(jnp.concatenate([w_gate, down_shard[:, :middle]], axis=1))
     feed_later = Box(jnp.concatenate([w_up, down_shard[:, middle:]], axis=1))
+    kin_parts = [
+        Box(w_gate),
+        Box(w_up),
+        Box(down_shard),
+    ]
     cot_own = Box(own_order(cotangent))
     x_own = Box(own_order(layer_in))
     slots = [Box(layer_in)]
@@ -1093,7 +1148,7 @@
         first.core()
         first.send()
         norm.send()
-        settle(slots[-1], first, norm, feed_first, feed_later, cot_own, x_own)
+        settle(slots[-1], first, norm, feed_first, feed_later, cot_own, x_own, *kin_parts)
     norm.rest()
     first.rest()
     first.core()
@@ -1105,11 +1160,6 @@
         return held
 
     x_own = x_own.value
-    kin_parts = [
-        Box(feed_first.value[:, :quarter_width]),
-        Box(feed_later.value[:, :quarter_width]),
-        Box(jnp.concatenate([v.value[:, quarter_width:] for v in (feed_first, feed_later)], axis=1)),
-    ]
     packs = [Many(*kin(kin_parts[0].value)[1:])]
     cot_far = Box(swap_head(cot_own.value, 1))
     feeds = [Gather(feed_first.value, feed_later.value)]
@@ -1155,7 +1205,7 @@
 
     total = Box(out_part([1]))
     gated = Box(gated_low)
-    settle(total, feeds[0], packs[2], gated)
+    settle(packs[2], total, feeds[0], gated)
     gated_low = gated.value
     quarters = 1 + len(packs[0].value)
     parts = Box(out_part(range(2, count_head + 1)))
@@ -1206,39 +1256,39 @@
     cot = Many(cot_own, cot_far)
     inner = Many(beside(inner_own), beside(inner_far))
     grads = [Many(a, b) for a, b in zip(grads_own, grads_far)]
-    early_sum = Scatter(second.value, grads[0].value)
-    early_sum.core()
-    early_sum.near()
     late_sums = [Scatter(second.value, g.value) for g in grads[1:]]
-    settle(grad_far, early_sum, *late_sums, cot, inner)
+    down_sum = Scatter(cot.value, inner.value)
+    settle(grad_far, *late_sums, down_sum, second, grads[0], down_far)
     second_grad = fed[-2] + grad_far.value.astype(wide)
     _, second_back = jax.vjp(layer_norm, hidden, gain_two, shift_two)
     hidden_part, gain_two_part, shift_two_part = second_back(second_grad)
     grad_hidden = cot_own.astype(wide) + hidden_part
 
     slots = [Box(grad_hidden.astype(low))]
-    settle(slots[0], early_sum, *late_sums, cot, inner)
+    settle(slots[0], *late_sums, down_sum, second, grads[0], down_far)
+    waits = [*late_sums, down_sum, down_far]
     passing = []
     for turn in range(count_head):
         rows = slots[-1]
         if turn < count_head - 1:
             slots.append(Box(ring_step(rows.value)))
         if turn == 0:
-            early_sum.send(True)
-            for thing in late_sums:
+            for thing in [*late_sums, down_sum]:
                 thing.core()
                 thing.near()
-            down_sum = Scatter(cot.value, inner.value)
-            waits = [early_sum, *late_sums, down_sum]
+            early_sum = Scatter(second.value, grads[0].value)
+            waits.append(early_sum)
         elif turn == 1:
             for thing in late_sums:
                 thing.send()
-            down_sum.core()
-            down_sum.near()
+            early_sum.core()
         elif turn == 2:
+            send_together(down_sum, late_sums[0])
             for thing in late_sums:
                 thing.rest()
-            down_sum.send()
+            early_sum.near()
+            down_far = Box(swap_head(down_far.value, 1))
+            waits.append(down_far)
         passing = gate_back(
             rows.value,
             first_full,
@@ -1255,7 +1305,7 @@
         )
         if turn < count_head - 1:
             passing = Many(*passing)
-            settle(slots[-1], *waits, cot, inner, passing)
+            settle(slots[-1], *waits, passing)
             passing = passing.value
     swish_grad, retained_grad, *crossed = passing
 
@@ -1275,34 +1325,32 @@
     for turn, rows in enumerate(slots):
         branch_low = lax.dynamic_update_slice_in_dim(branch_low, rows.value, start[turn], 0)
     branch, gated = Box(branch_low), Box(gated_low)
+    cut = 3 * quarter_width // 4
+    gates = [thing.rest()[0].astype(low) for thing in late_sums]
     ups = [thing.rest()[1].astype(low) for thing in late_sums]
-    early = [
-        Many(
-            *kin_sum(
-                [
-                    jnp.concatenate([thing.rest()[0].astype(low), up[:, :middle]], axis=1)
-                    for thing, up in zip(late_sums, ups)
-                ]
-            )
-        )
-    ]
-    ups = Many(*[up[:, middle:] for up in ups])
+    early = [Many(*kin_sum([gate[:, :cut] for gate in gates]))]
+    kin_next = Many(
+        *[beside([gate[:, cut:], up[:, :cut]]) for gate, up in zip(gates, ups)]
+    )
+    ups = Many(*[up[:, cut:] for up in ups])
     passed = Gather(*crossed)
     swish = Box(swish_grad)
-    settle(passed, early_sum, down_sum, ups, branch, gated, swish)
+    settle(passed, early_sum, down_sum, ups, kin_next, branch, gated, swish)
     passed.send()
-    settle(passed, down_sum, ups, swish)
-    passed.rest()
+    settle(passed, early[0], down_sum, ups, kin_next, swish, branch, gated)
+    early.append(Many(*kin_sum(kin_next.value)))
+    passed.rest_grouped()
     down_sum.rest()
     swish_sum = Scatter([normed], [swish.value])
-    settle(passed, early[0], early_sum, down_sum, ups, swish_sum)
+    out_sum = Scatter([branch.value], [gated.value])
+    settle(passed, early[1], early_sum, down_sum, ups, swish_sum, out_sum)
     passed.core()
     down_parts = jnp.split(jnp.concatenate(down_sum.rest(), axis=1), quarters, axis=1)
     early.append(
         Many(
             *kin_sum(
                 [
-                    jnp.concatenate([up, part.astype(low)], axis=1)
+                    beside([up, part.astype(low)])
                     for up, part in zip(ups.value, down_parts[1:])
                 ]
             )
@@ -1329,54 +1377,57 @@
 
     total, norm_sums = normed_part([1], backs)
     total, backs, norm_sums = Box(total), Box(backs), Box(norm_sums)
-    settle(total, early_sum, swish_sum, backs, norm_sums, branch, gated, down_far, early[1])
-    parts, more_sums = normed_part(range(2, count_head + 1), backs.value)
-    parts = Box(parts)
-    more_sums = Box(more_sums)
-    waits = [early_sum]
+    settle(total, early_sum, swish_sum, out_sum, backs, norm_sums, early[2])
+    parts, more_sums = normed_part([2], backs.value)
+    parts = [Box(parts)]
+    norm_sums = Many(norm_sums.value, more_sums)
     for turn in range(2, count_head + 1):
         got = ring_step(total.value)
         if turn == 2:
             early_sum.rest()
+            out_sum.core()
             swish_sum.near()
-            swish_sum.send(True)
             back_sum = Scatter([normed], [backs.value])
             back_sum.core()
             back_sum.near()
-            waits = [early_sum, swish_sum, back_sum, more_sums]
+            waits = [early_sum, swish_sum, back_sum, out_sum]
         elif turn == 3:
             back_sum.send()
-            out_sum = Scatter([branch.value], [gated.value])
-            out_sum.core()
+            swish_sum.send(True)
             out_sum.near()
-            waits = [swish_sum, back_sum, out_sum, more_sums]
+            later_parts, more_sums = normed_part(range(3, count_head + 1), backs.value)
+            parts.append(Box(later_parts))
+            norm_sums = Many(*norm_sums.value, more_sums)
+            waits = [swish_sum, back_sum, out_sum]
         elif turn == 4:
             back_sum.rest()
-            swish_sum.rest()
-            norm_sums = norm_sums.value + more_sums.value
+            out_sum.send(True)
             norm_sums = true_order(
-                jnp.concatenate([norm_sums, jnp.stack([gain_two_part, shift_two_part])])
+                jnp.concatenate(
+                    [sum(norm_sums.value), jnp.stack([gain_two_part, shift_two_part])]
+                )
             )
-            norm_sums = Box(sum_others(norm_sums, "sq", [1]))
-            waits = [back_sum, swish_sum, out_sum, norm_sums]
-        total = Box(add_rows(parts.value, turn - 2, got, low if turn < count_head else wide))
-        settle(total, *waits, parts, branch, gated, down_far)
-    down_far = swap_head(down_far.value, 1)
+            norm_sums = Many(sum_others(norm_sums, "sq", [1]))
+            waits = [back_sum, swish_sum, out_sum]
+        part = (parts[0], 0) if turn == 2 else (parts[1], turn - 3)
+        total = Box(
+            add_rows(part[0].value, part[1], got, low if turn < count_head else wide)
+        )
+        settle(total, *waits, *parts, norm_sums, backs)
     _, first_back = jax.vjp(lambda v: layer_norm(v, gain_one, shift_one), x_own.astype(wide))
     grad_in = grad_hidden + first_back(total.value)[0]
-    norm_sums = sum_others(norm_sums.value, "sq", range(2, count_sq, 2))
+    norm_sums = sum_others(norm_sums.value[0], "sq", range(2, count_sq, 2))
     norm_sums = sum_others(norm_sums, "head", range(1, count_head))
     first_sum, later_sum = early_sum.rest()
     early = [sum(p.astype(wide) for p in e.value) for e in early]
-    grad_gate = first_sum + early[0][:, :quarter_width]
-    grad_up = later_sum + jnp.concatenate(
-        [early[0][:, quarter_width:], early[1][:, :middle]], axis=1
-    )
-    grad_down = (down_parts[0] + early[1][:, middle:]).T
+    early = jnp.concatenate(early, axis=1)
+    grad_gate = first_sum + early[:, :quarter_width]
+    grad_up = later_sum + early[:, quarter_width : 2 * quarter_width]
+    grad_down = (down_parts[0] + early[:, 2 * quarter_width :]).T
     grad_value, grad_key_query = back_sum.rest()
     grad_swish = jnp.concatenate(swish_sum.rest(), axis=1)
     grad_out = jnp.concatenate(out_sum.rest(), axis=1).T
-    result = (hidden + fed[-1] + down_far.astype(wide)).astype(low)
+    result = (hidden + fed[-1] + down_far.value.astype(wide)).astype(low)
 
     piece = depth // (count_sq * count_head)
     first_norm = lax.dynamic_slice_in_dim(

time: 755 us -> 727 us (0.963)
  waiting for transfers between devices: 264 us -> 204 us
  local copies, waits for them, and re-layouts: 112 us -> 132 us
  Pallas kernels: 259 us -> 273 us
    ppermute x12, waiting for transfers between devices: 94.3 us -> 73.3 us  [ring_step(): lax.ppermute(value, 'head', [(i, (i + 1) % count) for i in range(count)])]
    ppermute x74 -> x70, waiting for transfers between devices: 128 us -> 107 us  [flip(): return lax.ppermute(value, 'sq', [(i, i ^ mask) for i in range(count)])]
    ppermute x9 -> x10, waiting for transfers between devices: 38.1 us -> 21 us  [swap_head(): return lax.ppermute(value, 'head', [(i, i ^ mask) for i in range(count)])]
    unnamed x429 -> x471, local copies, waits for them, and re-layouts: 90.3 us -> 104 us
    ppermute x74 -> x70, starting transfers between devices: 63.9 us -> 58.9 us  [flip(): return lax.ppermute(value, 'sq', [(i, i ^ mask) for i in range(count)])]
    pallas_call x4 -> x5, Pallas kernels: 39.7 us -> 44.1 us  [rows_back(): pl.pallas_call(functools.partial(rows_kernel, parts, sides, int(xhat is n...]
    pallas_call x11 -> x13, Pallas kernels: 15.3 us -> 15.4 us  [stack(): pl.pallas_call(stack_kernel, in_specs=[vmem] * len(pieces), out_specs=vme...]
  transfers between devices with their start and end apart: 102 -> 99, of which waited for: 38 -> 40; matrix products, arithmetic and copies ran while one was open for 8% -> 9% of each run, Pallas kernels for 26% -> 32%
where the time goes in v1:
time: 727 us; the launch traced here: 716 us
  Pallas kernels  273 us (38%)
  waiting for transfers between devices  204 us (28%)
  local copies, waits for them, and re-layouts  132 us (18%)
  starting transfers between devices  83.6 us (11%)
  other arithmetic  20.3 us (3%)
    ppermute x70, waiting for transfers between devices, flip(): return lax.ppermute(value, 'sq', [(i, i ^ mask) for i in range(count)])  107 us
    unnamed x471, local copies, waits for them, and re-layouts  104 us
    pallas_call x12, Pallas kernels, outer_half(): call(functools.partial(outer_kernel, len(lefts), len(extra), rows, bits),...  74.2 us
    ppermute x12, waiting for transfers between devices, ring_step(): lax.ppermute(value, 'head', [(i, (i + 1) % count) for i in range(count)])  73.3 us
    ppermute x70, starting transfers between devices, flip(): return lax.ppermute(value, 'sq', [(i, i ^ mask) for i in range(count)])  58.9 us
    pallas_call x5, Pallas kernels, rows_back(): pl.pallas_call(functools.partial(rows_kernel, parts, sides, int(xhat is n...  44.1 us
    pallas_call x3, Pallas kernels, feed_part(): pl.pallas_call(functools.partial(feed_kernel, top, quarter, places, sizes...  41.9 us
    pallas_call x4, Pallas kernels, gate_back(): pl.pallas_call(functools.partial(gate_back_kernel, heads, not prior, last...  24.5 us
  transfers between devices with their start and end apart: 99, of which 40 were waited for; matrix products, arithmetic and copies ran while one was open for 9% of the time, Pallas kernels for 32%

profile of v1, /device:TPU:0, one launch (start us, length us, event | category | flops | bytes accessed | tf_op | source)
XLA Modules:
  0.0 715.9 jit_solution(11946452465771648744)
XLA Ops:
  34.2 3.3 collective-permute-done.refs_1_
  40.0 22.6 %collective-permute-done.8 = bf16[2,4,256]{2,1,0:T(4,128)(2,1)S(1)} collective-permute-done((bf16[2,4,256]{2,1,0:T(4,128)(2,1)S(1)}, bf16[2,4,256]{2,1,0:T(4,128)(2,1)S(1)}, u32[]{:S(2)}, u32[]{:S(2)}) %collective-permute-start.8) | collective-permute-done | bytes 4128 | tf_op jit(solution)/shard_map/ppermute | solution.py:33
  70.1 23.2 %collective-permute-done.13 = bf16[4,4,256]{2,1,0:T(4,128)(2,1)S(1)} collective-permute-done((bf16[4,4,256]{2,1,0:T(4,128)(2,1)S(1)}, bf16[4,4,256]{2,1,0:T(4,128)(2,1)S(1)}, u32[]{:S(2)}, u32[]{:S(2)}) %collective-permute-start.13) | collective-permute-done | bytes 8224 | tf_op jit(solution)/shard_map/ppermute | solution.py:33
  109.7 16.0 %shard_map.248 = (bf16[1024,2048]{1,0:T(8,128)(2,1)}, bf16[1024,2048]{1,0:T(8,128)(2,1)}, bf16[1024,1536]{1,0:T(8,128)(2,1)}, bf16[2048,2048]{1,0:T(8,128)(2,1)}) custom-call(s32[8]{0:T(128)S(1)} %stack.126.order, s32[4]{0:T(128)S(1)} %pad_add_fusion.1.start, bf16[256,2048]{1,0:T(8,128)(2,1)} %refs_0_, bf16[256,2048]{1,0:T(8,128)(2,1)} %collective-permute-done.refs_1_, ...), custom_call_target="tpu_custom_call" | custom-call | flops 1 | bytes 1 | tf_op jit(solution)/shard_map/pallas_call | solution.py:590
  150.0 10.9 %shard_map.250 = (bf16[1024,1536]{1,0:T(8,128)(2,1)S(1)}, bf16[2048,2048]{1,0:T(8,128)(2,1)S(1)}) custom-call(bf16[1024,2048]{1,0:T(8,128)(2,1)S(1)} %copy-done.10, bf16[256,2048]{1,0:T(8,128)(2,1)S(1)} %copy-done.27, bf16[256,2048]{1,0:T(8,128)(2,1)} %collective-permute-done.1.refs_0_.refs_6_.refs_1_, bf16[256,2048]{1,0:T(8,128)(2,1)S(1)} %copy-done.44, ...), custom_call_target="tpu_custom_call" | custom-call | flops 1 | bytes 1 | tf_op jit(solution)/shard_map/pallas_call | solution.py:626
  160.9 3.2 copy-done
  176.7 4.0 shard_map.252.first_ref
  182.0 4.9 shard_map.253
  192.0 5.1 shard_map.254
  199.1 3.2 shard_map.258
  205.2 8.2 %shard_map.256.whole_ref = bf16[768,2048]{1,0:T(8,128)(2,1)} custom-call(s32[3]{0:T(128)} %and_select_fusion.1.begin_ref, bf16[1024,1024]{1,0:T(8,128)(2,1)} %copy-done.4, bf16[1024,1024]{1,0:T(8,128)(2,1)} %copy-done.4, bf16[1024,1024]{1,0:T(8,128)(2,1)} %copy-done.4, bf16[1024,1024]{1,0:T(8,128)(2,1)} %copy-done.4, bf16[1024,1024]{1,0:T(8,128)(2,1)} %copy-done.4, ...), custom_call_target="tpu_custom_call" | custom-call | flops 1 | bytes 1 | tf_op jit(solution)/shard_map/pallas_call | solution.py:843
  215.8 14.3 %collective-permute-done.31.got_ref = bf16[256,2048]{1,0:T(8,128)(2,1)S(1)} collective-permute-done((bf16[256,2048]{1,0:T(8,128)(2,1)}, bf16[256,2048]{1,0:T(8,128)(2,1)S(1)}, u32[]{:S(2)}, u32[]{:S(2)}) %collective-permute-start.31) | collective-permute-done | bytes 1048608 | tf_op jit(solution)/shard_map/ppermute | solution.py:256
  233.8 25.4 %collective-permute-done.35.got_ref = bf16[256,2048]{1,0:T(8,128)(2,1)S(1)} collective-permute-done((bf16[256,2048]{1,0:T(8,128)(2,1)S(1)}, bf16[256,2048]{1,0:T(8,128)(2,1)S(1)}, u32[]{:S(2)}, u32[]{:S(2)}) %collective-permute-start.35) | collective-permute-done | bytes 1048608 | tf_op jit(solution)/shard_map/ppermute | solution.py:256
  262.5 23.9 %collective-permute-done.40.got_ref = bf16[256,2048]{1,0:T(8,128)(2,1)S(1)} collective-permute-done((bf16[256,2048]{1,0:T(8,128)(2,1)S(1)}, bf16[256,2048]{1,0:T(8,128)(2,1)S(1)}, u32[]{:S(2)}, u32[]{:S(2)}) %collective-permute-start.40) | collective-permute-done | bytes 1048608 | tf_op jit(solution)/shard_map/ppermute | solution.py:256
  291.8 9.5 %shard_map.264 = (bf16[256,1024]{1,0:T(8,128)(2,1)S(1)}, bf16[256,2048]{1,0:T(8,128)(2,1)S(1)}, f32[256,2048]{1,0:T(8,128)S(1)}, f32[256,2048]{1,0:T(8,128)S(1)}) custom-call(bf16[256,2048]{1,0:T(8,128)(2,1)S(1)} %add_convert_fusion.1.second_ref.refs_0_, bf16[256,2048]{1,0:T(8,128)(2,1)S(1)} %copy-done.17, bf16[256,1536]{1,0:T(8,128)(2,1)} %get-tuple-element.645.refs_0_, ...), custom_call_target="tpu_custom_call" | custom-call | flops 1 | bytes 1 | tf_op jit(solution)/shard_map/pallas_call | solution.py:726
  305.8 3.8 collective-permute-done.44.refs_0_.refs_14_.refs_3_
  310.0 5.3 collective-permute-done.43.second_ref.refs_1_
  315.5 3.4 collective-permute-done.47.refs_21_.refs_10_
  320.0 21.3 %shard_map.266 = (bf16[256,1024]{1,0:T(8,128)(2,1)S(1)}, bf16[256,2048]{1,0:T(8,128)(2,1)}, bf16[256,1024]{1,0:T(8,128)(2,1)S(1)}, bf16[256,2048]{1,0:T(8,128)(2...) custom-call(bf16[256,2048]{1,0:T(8,128)(2,1)} %copy-done.23, ...), custom_call_target="tpu_custom_call" | custom-call | flops 1 | bytes 1 | tf_op jit(solution)/shard_map/pallas_call | solution.py:726
  347.2 11.1 %shard_map.267 = (bf16[256,1024]{1,0:T(8,128)(2,1)S(1)}, bf16[256,2048]{1,0:T(8,128)(2,1)S(1)}, f32[256,2048]{1,0:T(8,128)S(1)}, f32[256,2048]{1,0:T(8,128)S(1)}) custom-call(bf16[256,2048]{1,0:T(8,128)(2,1)S(1)} %add_convert_fusion.1.second_ref.refs_0_, bf16[256,2048]{1,0:T(8,128)(2,1)S(1)} %copy-done.17, ...), custom_call_target="tpu_custom_call" | custom-call | flops 1 | bytes 1 | tf_op jit(solution)/shard_map/pallas_call | solution.py:726
  358.4 6.6 shard_map.271
  365.1 4.8 shard_map.268
  374.5 6.0 shard_map.275
  380.5 4.8 shard_map.274
  385.2 6.1 shard_map.273
  395.3 6.7 shard_map.272
  406.4 6.3 shard_map.277
  412.7 17.2 %collective-permute-done.53.refs_1_ = bf16[512,1024]{1,0:T(8,128)(2,1)} collective-permute-done((bf16[512,1024]{1,0:T(8,128)(2,1)}, bf16[512,1024]{1,0:T(8,128)(2,1)}, u32[]{:S(2)}, u32[]{:S(2)}) %collective-permute-start.53) | collective-permute-done | bytes 1048608 | tf_op jit(solution)/shard_map/ppermute | solution.py:33
  445.5 6.7 shard_map.282
  454.2 6.1 shard_map.283
  462.7 7.7 %collective-permute-done.58 = bf16[768,1024]{1,0:T(8,128)(2,1)} collective-permute-done((bf16[768,1024]{1,0:T(8,128)(2,1)}, bf16[768,1024]{1,0:T(8,128)(2,1)}, u32[]{:S(2)}, u32[]{:S(2)}) %collective-permute-start.58) | collective-permute-done | bytes 1572896 | tf_op jit(solution)/shard_map/ppermute | solution.py:33
  478.9 5.6 collective-permute-done.59
  488.0 6.1 shard_map.284
  498.6 4.6 collective-permute-done.60.refs_1_.refs_2_
  510.3 4.6 shard_map.289
  514.9 5.9 shard_map.290
  521.4 6.9 collective-permute-done.64
  529.4 3.4 collective-permute-done.65
  538.8 4.0 shard_map.292.last_ref
  549.1 6.3 shard_map.293.refs_0_.refs_2_.refs_1_.refs_3_.refs_5_
  557.4 9.1 %shard_map.294 = (bf16[256,2048]{1,0:T(8,128)(2,1)}, f32[2,2048]{1,0:T(2,128)}) custom-call(s32[1]{0:T(128)S(6)} %select_n.216.begin_ref, bf16[1024,2048]{1,0:T(8,128)(2,1)} %copy-done.1, bf16[1024,1024]{1,0:T(8,128)(2,1)} %get-tuple-element.811.refs_1_.refs_4_, bf16[1024,2048]{1,0:T(8,128)(2,1)} %copy-done.1, ...), custom_call_target="tpu_custom_call" | custom-call | flops 1 | bytes 1 | tf_op jit(solution)/shard_map/pallas_call | solution.py:843
  570.4 7.2 %shard_map.301 = bf16[1024,2048]{1,0:T(8,128)(2,1)} custom-call(bf16[1024,2048]{1,0:T(8,128)(2,1)S(1)} %copy-done.12, bf16[1024,2048]{1,0:T(8,128)(2,1)S(1)} %copy-done.2), custom_call_target="tpu_custom_call" | custom-call | flops 1 | bytes 1 | tf_op jit(solution)/shard_map/pallas_call | solution.py:792
  589.2 5.5 shard_map.300
  597.0 9.0 %shard_map.296 = (bf16[256,2048]{1,0:T(8,128)(2,1)}, f32[2,2048]{1,0:T(2,128)}) custom-call(s32[1]{0:T(128)S(6)} %select_n.243.begin_ref, bf16[1024,2048]{1,0:T(8,128)(2,1)} %copy-done.1, bf16[1024,1024]{1,0:T(8,128)(2,1)} %get-tuple-element.811.refs_1_.refs_4_, bf16[1024,2048]{1,0:T(8,128)(2,1)} %copy-done.1, ...), custom_call_target="tpu_custom_call" | custom-call | flops 1 | bytes 1 | tf_op jit(solution)/shard_map/pallas_call | solution.py:843
  614.5 8.9 %shard_map.302 = (bf16[512,1024]{1,0:T(8,128)(2,1)S(1)}, bf16[512,1024]{1,0:T(8,128)(2,1)}, bf16[512,1024]{1,0:T(8,128)(2,1)S(1)}, bf16[512,1024]{1,0:T(8,128)(2,1)}) custom-call(bf16[1024,2048]{1,0:T(8,128)(2,1)S(1)} %copy-done.14, bf16[1024,2048]{1,0:T(8,128)(2,1)S(1)} %copy-done.3, bf16[1024,2048]{1,0:T(8,128)(2,1)} %collective-permute-done.76.refs_2_), custom_call_target="tpu_custom_call" | custom-call | flops 1 | bytes 1 | tf_op jit(solution)/shard_map/pallas_call | solution.py:792
  631.9 6.6 shard_map.306
  640.1 12.7 %shard_map.303 = (bf16[512,2048]{1,0:T(8,128)(2,1)}, f32[2,2048]{1,0:T(2,128)}) custom-call(s32[2]{0:T(128)} %and_select_fusion.begin_ref, bf16[1024,2048]{1,0:T(8,128)(2,1)} %copy-done.1, bf16[1024,1024]{1,0:T(8,128)(2,1)} %get-tuple-element.811.refs_1_.refs_4_, bf16[1024,2048]{1,0:T(8,128)(2,1)} %copy-done.1, bf16[1024,2048]{1,0:T(8,128)(2,1)} %copy-done.1, ...), custom_call_target="tpu_custom_call" | custom-call | flops 1 | bytes 1 | tf_op jit(solution)/shard_map/pallas_call | solution.py:843
  686.3 3.5 collective-permute-done.86.refs_1_
  (780 shorter events, 301.1 us)
Async XLA Ops:
  3.7 30.4 %collective-permute-start.1 = (bf16[256,2048]{1,0:T(8,128)(2,1)S(1)}, bf16[256,2048]{1,0:T(8,128)(2,1)}, u32[]{:S(2)}, u32[]{:S(2)}) collective-permute-start(bf16[256,2048]{1,0:T(8,128)(2,1)S(1)} %get-tuple-element.520.refs_0_.refs_5_), channel_id=1, source_target_pairs={{0,2},{1,3},{2,0},{3,1},{4,6},{5,7},{6,4},{7,5},{8,10},{9,11},{10,... | collective-permute-start | bytes 3145736 | tf_op jit(solution)/shard_map/ppermute | solution.py:33
  6.8 27.4 %collective-permute-start.2 = (bf16[256,2048]{1,0:T(8,128)(2,1)S(1)}, bf16[256,2048]{1,0:T(8,128)(2,1)}, u32[]{:S(2)}, u32[]{:S(2)}) collective-permute-start(bf16[256,2048]{1,0:T(8,128)(2,1)S(1)} %get-tuple-element.524.refs_1_.refs_9_.refs_4_), channel_id=1, source_target_pairs={{0,4},{1,5},{2,6},{3,7},{4,0},{5,1},{6,2},{7,3},{8,12},{9,13},{10,... | collective-permute-start | bytes 3145736 | tf_op jit(solution)/shard_map/ppermute | solution.py:33
  9.7 27.8 %collective-permute-start.3 = (bf16[2,256,2048]{2,1,0:T(8,128)(2,1)}, bf16[2,256,2048]{2,1,0:T(8,128)(2,1)}, u32[]{:S(2)}, u32[]{:S(2)}) collective-permute-start(bf16[2,256,2048]{2,1,0:T(8,128)(2,1)} %shard_map.245), channel_id=1, source_target_pairs={{0,1},{1,0},{2,3},{3,2},{4,5},{5,4},{6,7},{7,6},{8,9},{9,8},{10,11... | collective-permute-start | bytes 6291464 | tf_op jit(solution)/shard_map/ppermute | solution.py:33
  9.7 27.7 %collective-permute-start = (bf16[256,2048]{1,0:T(8,128)(2,1)}, bf16[256,2048]{1,0:T(8,128)(2,1)}, u32[]{:S(2)}, u32[]{:S(2)}) collective-permute-start(bf16[256,2048]{1,0:T(8,128)(2,1)} %refs_0_), channel_id=1, source_target_pairs={{0,8},{8,16},{16,24},{24,0},{1,9},{9,17},{17,25},{25,1},{2,10},{10... | collective-permute-start | bytes 3145736 | tf_op jit(solution)/shard_map/ppermute | solution.py:256
  37.5 26.9 %collective-permute-start.5 = (bf16[256,2048]{1,0:T(8,128)(2,1)}, bf16[256,2048]{1,0:T(8,128)(2,1)S(1)}, u32[]{:S(2)}, u32[]{:S(2)}) collective-permute-start(bf16[256,2048]{1,0:T(8,128)(2,1)} %collective-permute-done.refs_1_), channel_id=1, source_target_pairs={{0,8},{8,16},{16,24},{24,0},{1,9},{9,17},{17,25},{25,1},{2,10},{10... | collective-permute-start | bytes 3145736 | tf_op jit(solution)/shard_map/ppermute | solution.py:256
  37.5 26.9 %collective-permute-start.6 = (bf16[256,2048]{1,0:T(8,128)(2,1)S(1)}, bf16[256,2048]{1,0:T(8,128)(2,1)S(1)}, u32[]{:S(2)}, u32[]{:S(2)}) collective-permute-start(bf16[256,2048]{1,0:T(8,128)(2,1)S(1)} %get-tuple-element.520.refs_0_.refs_5_), channel_id=1, source_target_pairs={{0,4},{1,5},{2,6},{3,7},{4,0},{5,1},{6,2},{7,3},{8,12},{9,13},{10,... | collective-permute-start | bytes 3145736 | tf_op jit(solution)/shard_map/ppermute | solution.py:33
  67.3 29.0 %collective-permute-start.12 = (bf16[4,256,2048]{2,1,0:T(8,128)(2,1)S(1)}, bf16[4,256,2048]{2,1,0:T(8,128)(2,1)}, u32[]{:S(2)}, u32[]{:S(2)}) collective-permute-start(bf16[4,256,2048]{2,1,0:T(8,128)(2,1)S(1)} %shard_map.246), channel_id=1, source_target_pairs={{0,1},{1,0},{2,3},{3,2},{4,5},{5,4},{6,7},{7,6},{8,9},{9,8},{10,11... | collective-permute-start | bytes 12582920 | tf_op jit(solution)/shard_map/ppermute | solution.py:33
  68.7 26.7 %collective-permute-start.9 = (bf16[256,2048]{1,0:T(8,128)(2,1)S(1)}, bf16[256,2048]{1,0:T(8,128)(2,1)S(1)}, u32[]{:S(2)}, u32[]{:S(2)}) collective-permute-start(bf16[256,2048]{1,0:T(8,128)(2,1)S(1)} %collective-permute-done.5.refs_2_), channel_id=1, source_target_pairs={{0,8},{8,16},{16,24},{24,0},{1,9},{9,17},{17,25},{25,1},{2,10},{10... | collective-permute-start | bytes 3145736 | tf_op jit(solution)/shard_map/ppermute | solution.py:256
  97.9 36.9 %collective-permute-start.16 = (bf16[256,2048]{1,0:T(8,128)(2,1)S(1)}, bf16[256,2048]{1,0:T(8,128)(2,1)}, u32[]{:S(2)}, u32[]{:S(2)}) collective-permute-start(bf16[256,2048]{1,0:T(8,128)(2,1)S(1)} %dynamic-slice_dynamic-update-slice_fusion.24.cot_ref.refs_0_), channel_id=1, source_target_pairs={{0,8},{8,0},{16,24},{24,16},{1,9},{9,1},{17,25},{25,17},{2,10},{10... | collective-permute-start | bytes 3145736 | tf_op jit(solution)/shard_map/ppermute | solution.py:301
  98.1 34.4 %collective-permute-start.17 = (bf16[256,1536]{1,0:T(8,128)(2,1)}, bf16[256,1536]{1,0:T(8,128)(2,1)S(1)}, u32[]{:S(2)}, u32[]{:S(2)}) collective-permute-start(bf16[256,1536]{1,0:T(8,128)(2,1)} %get-tuple-element.645.refs_0_), channel_id=1, source_target_pairs={{0,2},{1,3},{2,0},{3,1},{4,6},{5,7},{6,4},{7,5},{8,10},{9,11},{10,... | collective-permute-start | bytes 2359304 | tf_op jit(solution)/shard_map/ppermute | solution.py:33
  99.5 34.0 %collective-permute-start.18 = (bf16[256,1536]{1,0:T(8,128)(2,1)}, bf16[256,1536]{1,0:T(8,128)(2,1)S(1)}, u32[]{:S(2)}, u32[]{:S(2)}) collective-permute-start(bf16[256,1536]{1,0:T(8,128)(2,1)} %get-tuple-element.649.refs_1_.refs_4_), channel_id=1, source_target_pairs={{0,4},{1,5},{2,6},{3,7},{4,0},{5,1},{6,2},{7,3},{8,12},{9,13},{10,... | collective-permute-start | bytes 2359304 | tf_op jit(solution)/shard_map/ppermute | solution.py:33
  101.0 31.5 %collective-permute-start.15 = (bf16[256,1024]{1,0:T(8,128)(2,1)}, bf16[256,1024]{1,0:T(8,128)(2,1)S(1)}, u32[]{:S(2)}, u32[]{:S(2)}) collective-permute-start(bf16[256,1024]{1,0:T(8,128)(2,1)} %param.24), channel_id=1, source_target_pairs={{0,16},{8,24},{16,0},{24,8},{1,17},{9,25},{17,1},{25,9},{2,18},{10... | collective-permute-start | bytes 1572872 | tf_op jit(solution)/shard_map/ppermute | solution.py:301
  137.7 26.6 %collective-permute-start.25 = (bf16[256,1024]{1,0:T(8,128)(2,1)S(1)}, bf16[256,1024]{1,0:T(8,128)(2,1)S(1)}, u32[]{:S(2)}, u32[]{:S(2)}) collective-permute-start(bf16[256,1024]{1,0:T(8,128)(2,1)S(1)} %copy-done.195), channel_id=1, source_target_pairs={{0,16},{8,24},{16,0},{24,8},{1,17},{9,25},{17,1},{25,9},{2,18},{10... | collective-permute-start | bytes 1572872 | tf_op jit(solution)/shard_map/ppermute | solution.py:301
  170.4 28.7 %collective-permute-start.30 = (bf16[2,256,1536]{2,1,0:T(8,128)(2,1)}, bf16[2,256,1536]{2,1,0:T(8,128)(2,1)}, u32[]{:S(2)}, u32[]{:S(2)}) collective-permute-start(bf16[2,256,1536]{2,1,0:T(8,128)(2,1)} %shard_map.255), channel_id=1, source_target_pairs={{0,1},{1,0},{2,3},{3,2},{4,5},{5,4},{6,7},{7,6},{8,9},{9,8},{10,11... | collective-permute-start | bytes 4718600 | tf_op jit(solution)/shard_map/ppermute | solution.py:33
  170.9 28.2 %collective-permute-start.28 = (bf16[256,1536]{1,0:T(8,128)(2,1)}, bf16[256,1536]{1,0:T(8,128)(2,1)}, u32[]{:S(2)}, u32[]{:S(2)}) collective-permute-start(bf16[256,1536]{1,0:T(8,128)(2,1)} %get-tuple-element.645.refs_0_), channel_id=1, source_target_pairs={{0,4},{1,5},{2,6},{3,7},{4,0},{5,1},{6,2},{7,3},{8,12},{9,13},{10,... | collective-permute-start | bytes 2359304 | tf_op jit(solution)/shard_map/ppermute | solution.py:33
  172.4 26.7 %collective-permute-start.29 = (bf16[256,1536]{1,0:T(8,128)(2,1)}, bf16[256,1536]{1,0:T(8,128)(2,1)}, u32[]{:S(2)}, u32[]{:S(2)}) collective-permute-start(bf16[256,1536]{1,0:T(8,128)(2,1)} %get-tuple-element.649.refs_1_.refs_4_), channel_id=1, source_target_pairs={{0,2},{1,3},{2,0},{3,1},{4,6},{5,7},{6,4},{7,5},{8,10},{9,11},{10,... | collective-permute-start | bytes 2359304 | tf_op jit(solution)/shard_map/ppermute | solution.py:33
  202.3 28.4 %collective-permute-start.34 = (bf16[4,256,1536]{2,1,0:T(8,128)(2,1)}, bf16[4,256,1536]{2,1,0:T(8,128)(2,1)S(1)}, u32[]{:S(2)}, u32[]{:S(2)}) collective-permute-start(bf16[4,256,1536]{2,1,0:T(8,128)(2,1)} %shard_map.258), channel_id=1, source_target_pairs={{0,1},{1,0},{2,3},{3,2},{4,5},{5,4},{6,7},{7,6},{8,9},{9,8},{10,11... | collective-permute-start | bytes 9437192 | tf_op jit(solution)/shard_map/ppermute | solution.py:33
  202.3 27.8 %collective-permute-start.31 = (bf16[256,2048]{1,0:T(8,128)(2,1)}, bf16[256,2048]{1,0:T(8,128)(2,1)S(1)}, u32[]{:S(2)}, u32[]{:S(2)}) collective-permute-start(bf16[256,2048]{1,0:T(8,128)(2,1)} %shard_map.254), channel_id=1, source_target_pairs={{0,8},{8,16},{16,24},{24,0},{1,9},{9,17},{17,25},{25,1},{2,10},{10... | collective-permute-start | bytes 3145736 | tf_op jit(solution)/shard_map/ppermute | solution.py:256
  202.6 28.1 %collective-permute-start.32 = (bf16[256,1536]{1,0:T(8,128)(2,1)S(1)}, bf16[256,1536]{1,0:T(8,128)(2,1)S(1)}, u32[]{:S(2)}, u32[]{:S(2)}) collective-permute-start(bf16[256,1536]{1,0:T(8,128)(2,1)S(1)} %copy-done.51), channel_id=1, source_target_pairs={{0,4},{1,5},{2,6},{3,7},{4,0},{5,1},{6,2},{7,3},{8,12},{9,13},{10,... | collective-permute-start | bytes 2359304 | tf_op jit(solution)/shard_map/ppermute | solution.py:33
  203.3 27.4 %collective-permute-start.33 = (bf16[256,1536]{1,0:T(8,128)(2,1)S(1)}, bf16[256,1536]{1,0:T(8,128)(2,1)S(1)}, u32[]{:S(2)}, u32[]{:S(2)}) collective-permute-start(bf16[256,1536]{1,0:T(8,128)(2,1)S(1)} %copy-done.53), channel_id=1, source_target_pairs={{0,2},{1,3},{2,0},{3,1},{4,6},{5,7},{6,4},{7,5},{8,10},{9,11},{10,... | collective-permute-start | bytes 2359304 | tf_op jit(solution)/shard_map/ppermute | solution.py:33
  230.8 28.9 %collective-permute-start.39 = (bf16[2,256,1536]{2,1,0:T(8,128)(2,1)S(1)}, bf16[2,256,1536]{2,1,0:T(8,128)(2,1)S(1)}, u32[]{:S(2)}, u32[]{:S(2)}) collective-permute-start(bf16[2,256,1536]{2,1,0:T(8,128)(2,1)S(1)} %shard_map.261), channel_id=1, source_target_pairs={{0,1},{1,0},{2,3},{3,2},{4,5},{5,4},{6,7},{7,6},{8,9},{9,8},{10,11... | collective-permute-start | bytes 4718600 | tf_op jit(solution)/shard_map/ppermute | solution.py:33
  231.8 27.9 %collective-permute-start.36 = (bf16[2,256,1536]{2,1,0:T(8,128)(2,1)S(1)}, bf16[2,256,1536]{2,1,0:T(8,128)(2,1)S(1)}, u32[]{:S(2)}, u32[]{:S(2)}) collective-permute-start(bf16[2,256,1536]{2,1,0:T(8,128)(2,1)S(1)} %shard_map.260), channel_id=1, source_target_pairs={{0,1},{1,0},{2,3},{3,2},{4,5},{5,4},{6,7},{7,6},{8,9},{9,8},{10,11... | collective-permute-start | bytes 4718600 | tf_op jit(solution)/shard_map/ppermute | solution.py:33
  231.8 27.4 %collective-permute-start.35 = (bf16[256,2048]{1,0:T(8,128)(2,1)S(1)}, bf16[256,2048]{1,0:T(8,128)(2,1)S(1)}, u32[]{:S(2)}, u32[]{:S(2)}) collective-permute-start(bf16[256,2048]{1,0:T(8,128)(2,1)S(1)} %shard_map.257), channel_id=1, source_target_pairs={{0,8},{8,16},{16,24},{24,0},{1,9},{9,17},{17,25},{25,1},{2,10},{10... | collective-permute-start | bytes 3145736 | tf_op jit(solution)/shard_map/ppermute | solution.py:256
  231.8 27.9 %collective-permute-start.37 = (bf16[256,1536]{1,0:T(8,128)(2,1)S(1)}, bf16[256,1536]{1,0:T(8,128)(2,1)S(1)}, u32[]{:S(2)}, u32[]{:S(2)}) collective-permute-start(bf16[256,1536]{1,0:T(8,128)(2,1)S(1)} %pad_maximum_fusion.7.refs_0_.refs_11_), channel_id=1, source_target_pairs={{0,2},{1,3},{2,0},{3,1},{4,6},{5,7},{6,4},{7,5},{8,10},{9,11},{10,... | collective-permute-start | bytes 2359304 | tf_op jit(solution)/shard_map/ppermute | solution.py:33
  233.1 26.6 %collective-permute-start.38 = (bf16[256,1536]{1,0:T(8,128)(2,1)S(1)}, bf16[256,1536]{1,0:T(8,128)(2,1)S(1)}, u32[]{:S(2)}, u32[]{:S(2)}) collective-permute-start(bf16[256,1536]{1,0:T(8,128)(2,1)S(1)} %pad_maximum_fusion.8.refs_1_.refs_15_.refs_4_), channel_id=1, source_target_pairs={{0,4},{1,5},{2,6},{3,7},{4,0},{5,1},{6,2},{7,3},{8,12},{9,13},{10,... | collective-permute-start | bytes 2359304 | tf_op jit(solution)/shard_map/ppermute | solution.py:33
  259.8 26.6 %collective-permute-start.40 = (bf16[256,2048]{1,0:T(8,128)(2,1)S(1)}, bf16[256,2048]{1,0:T(8,128)(2,1)S(1)}, u32[]{:S(2)}, u32[]{:S(2)}) collective-permute-start(bf16[256,2048]{1,0:T(8,128)(2,1)S(1)} %shard_map.259), channel_id=1, source_target_pairs={{0,8},{8,16},{16,24},{24,0},{1,9},{9,17},{17,25},{25,1},{2,10},{10... | collective-permute-start | bytes 3145736 | tf_op jit(solution)/shard_map/ppermute | solution.py:256
  259.8 27.1 %collective-permute-start.41 = (bf16[256,1536]{1,0:T(8,128)(2,1)S(1)}, bf16[256,1536]{1,0:T(8,128)(2,1)S(1)}, u32[]{:S(2)}, u32[]{:S(2)}) collective-permute-start(bf16[256,1536]{1,0:T(8,128)(2,1)S(1)} %pad_maximum_fusion.7.refs_0_.refs_11_), channel_id=1, source_target_pairs={{0,4},{1,5},{2,6},{3,7},{4,0},{5,1},{6,2},{7,3},{8,12},{9,13},{10,... | collective-permute-start | bytes 2359304 | tf_op jit(solution)/shard_map/ppermute | solution.py:33
  260.5 26.4 %collective-permute-start.42 = (bf16[256,1536]{1,0:T(8,128)(2,1)S(1)}, bf16[256,1536]{1,0:T(8,128)(2,1)S(1)}, u32[]{:S(2)}, u32[]{:S(2)}) collective-permute-start(bf16[256,1536]{1,0:T(8,128)(2,1)S(1)} %pad_maximum_fusion.8.refs_1_.refs_15_.refs_4_), channel_id=1, source_target_pairs={{0,2},{1,3},{2,0},{3,1},{4,6},{5,7},{6,4},{7,5},{8,10},{9,11},{10,... | collective-permute-start | bytes 2359304 | tf_op jit(solution)/shard_map/ppermute | solution.py:33
  341.4 28.4 %collective-permute-start.48 = (bf16[256,2048]{1,0:T(8,128)(2,1)}, bf16[256,2048]{1,0:T(8,128)(2,1)S(1)}, u32[]{:S(2)}, u32[]{:S(2)}) collective-permute-start(bf16[256,2048]{1,0:T(8,128)(2,1)} %get-tuple-element.677), channel_id=1, source_target_pairs={{0,8},{8,0},{16,24},{24,16},{1,9},{9,1},{17,25},{25,17},{2,10},{10... | collective-permute-start | bytes 3145736 | tf_op jit(solution)/shard_map/ppermute | solution.py:301
  373.6 30.4 %collective-permute-start.49 = (bf16[256,2048]{1,0:T(8,128)(2,1)}, bf16[256,2048]{1,0:T(8,128)(2,1)}, u32[]{:S(2)}, u32[]{:S(2)}) collective-permute-start(bf16[256,2048]{1,0:T(8,128)(2,1)} %fusion.5.branch_ref), channel_id=1, source_target_pairs={{0,8},{8,16},{16,24},{24,0},{1,9},{9,17},{17,25},{25,1},{2,10},{10... | collective-permute-start | bytes 3145736 | tf_op jit(solution)/shard_map/ppermute | solution.py:256
  403.9 29.5 %collective-permute-start.55 = (bf16[1024,2048]{1,0:T(8,128)(2,1)}, bf16[1024,2048]{1,0:T(8,128)(2,1)}, u32[]{:S(2)}, u32[]{:S(2)}) collective-permute-start(bf16[1024,2048]{1,0:T(8,128)(2,1)} %shard_map.274), channel_id=1, source_target_pairs={{0,1},{1,0},{2,3},{3,2},{4,5},{5,4},{6,7},{7,6},{8,9},{9,8},{10,11... | collective-permute-start | bytes 12582920 | tf_op jit(solution)/shard_map/ppermute | solution.py:33
  405.9 27.5 %collective-permute-start.52 = (bf16[256,2048]{1,0:T(8,128)(2,1)}, bf16[256,2048]{1,0:T(8,128)(2,1)}, u32[]{:S(2)}, u32[]{:S(2)}) collective-permute-start(bf16[256,2048]{1,0:T(8,128)(2,1)} %collective-permute-done.49.branch_ref), channel_id=1, source_target_pairs={{0,8},{8,16},{16,24},{24,0},{1,9},{9,17},{17,25},{25,1},{2,10},{10... | collective-permute-start | bytes 3145736 | tf_op jit(solution)/shard_map/ppermute | solution.py:256
  434.7 35.7 %collective-permute-start.58 = (bf16[768,1024]{1,0:T(8,128)(2,1)}, bf16[768,1024]{1,0:T(8,128)(2,1)}, u32[]{:S(2)}, u32[]{:S(2)}) collective-permute-start(bf16[768,1024]{1,0:T(8,128)(2,1)} %shard_map.279), channel_id=1, source_target_pairs={{0,4},{1,5},{2,6},{3,7},{4,0},{5,1},{6,2},{7,3},{8,12},{9,13},{10,... | collective-permute-start | bytes 4718600 | tf_op jit(solution)/shard_map/ppermute | solution.py:33
  437.3 35.4 %collective-permute-start.57 = (bf16[768,1024]{1,0:T(8,128)(2,1)}, bf16[768,1024]{1,0:T(8,128)(2,1)}, u32[]{:S(2)}, u32[]{:S(2)}) collective-permute-start(bf16[768,1024]{1,0:T(8,128)(2,1)} %shard_map.278), channel_id=1, source_target_pairs={{0,2},{1,3},{2,0},{3,1},{4,6},{5,7},{6,4},{7,5},{8,10},{9,11},{10,... | collective-permute-start | bytes 4718600 | tf_op jit(solution)/shard_map/ppermute | solution.py:33
  438.1 40.8 %collective-permute-start.56 = (bf16[256,2048]{1,0:T(8,128)(2,1)}, bf16[256,2048]{1,0:T(8,128)(2,1)}, u32[]{:S(2)}, u32[]{:S(2)}) collective-permute-start(bf16[256,2048]{1,0:T(8,128)(2,1)} %collective-permute-done.52.branch_ref), channel_id=1, source_target_pairs={{0,8},{8,16},{16,24},{24,0},{1,9},{9,17},{17,25},{25,1},{2,10},{10... | collective-permute-start | bytes 3145736 | tf_op jit(solution)/shard_map/ppermute | solution.py:256
  438.1 46.4 %collective-permute-start.59 = (bf16[256,2048]{1,0:T(8,128)(2,1)}, bf16[256,2048]{1,0:T(8,128)(2,1)}, u32[]{:S(2)}, u32[]{:S(2)}) collective-permute-start(bf16[256,2048]{1,0:T(8,128)(2,1)} %get-tuple-element.752), channel_id=1, source_target_pairs={{0,8},{8,0},{16,24},{24,16},{1,9},{9,1},{17,25},{25,17},{2,10},{10... | collective-permute-start | bytes 3145736 | tf_op jit(solution)/shard_map/ppermute | solution.py:301
  534.3 33.9 %collective-permute-start.71 = (bf16[1024,1024]{1,0:T(8,128)(2,1)}, bf16[1024,1024]{1,0:T(8,128)(2,1)}, u32[]{:S(2)}, u32[]{:S(2)}) collective-permute-start(bf16[1024,1024]{1,0:T(8,128)(2,1)} %shard_map.289), channel_id=1, source_target_pairs={{0,1},{1,0},{2,3},{3,2},{4,5},{5,4},{6,7},{7,6},{8,9},{9,8},{10,11... | collective-permute-start | bytes 6291464 | tf_op jit(solution)/shard_map/ppermute | solution.py:33
  534.8 33.4 %collective-permute-start.69 = (bf16[512,1024]{1,0:T(8,128)(2,1)}, bf16[512,1024]{1,0:T(8,128)(2,1)}, u32[]{:S(2)}, u32[]{:S(2)}) collective-permute-start(bf16[512,1024]{1,0:T(8,128)(2,1)} %get-tuple-element.825), channel_id=1, source_target_pairs={{0,4},{1,5},{2,6},{3,7},{4,0},{5,1},{6,2},{7,3},{8,12},{9,13},{10,... | collective-permute-start | bytes 3145736 | tf_op jit(solution)/shard_map/ppermute | solution.py:33
  535.8 32.4 %collective-permute-start.70 = (bf16[512,1024]{1,0:T(8,128)(2,1)}, bf16[512,1024]{1,0:T(8,128)(2,1)}, u32[]{:S(2)}, u32[]{:S(2)}) collective-permute-start(bf16[512,1024]{1,0:T(8,128)(2,1)} %get-tuple-element.827), channel_id=1, source_target_pairs={{0,2},{1,3},{2,0},{3,1},{4,6},{5,7},{6,4},{7,5},{8,10},{9,11},{10,... | collective-permute-start | bytes 3145736 | tf_op jit(solution)/shard_map/ppermute | solution.py:33
  537.8 30.3 %collective-permute-start.72 = (bf16[256,1280]{1,0:T(8,128)(2,1)}, bf16[256,1280]{1,0:T(8,128)(2,1)}, u32[]{:S(2)}, u32[]{:S(2)}) collective-permute-start(bf16[256,1280]{1,0:T(8,128)(2,1)} %shard_map.295), channel_id=1, source_target_pairs={{0,16},{8,24},{16,0},{24,8},{1,17},{9,25},{17,1},{25,9},{2,18},{10... | collective-permute-start | bytes 1966088 | tf_op jit(solution)/shard_map/ppermute | solution.py:301
  577.6 34.7 %collective-permute-start.76 = (bf16[1024,2048]{1,0:T(8,128)(2,1)}, bf16[1024,2048]{1,0:T(8,128)(2,1)}, u32[]{:S(2)}, u32[]{:S(2)}) collective-permute-start(bf16[1024,2048]{1,0:T(8,128)(2,1)} %shard_map.301), channel_id=1, source_target_pairs={{0,1},{1,0},{2,3},{3,2},{4,5},{5,4},{6,7},{7,6},{8,9},{9,8},{10,11... | collective-permute-start | bytes 12582920 | tf_op jit(solution)/shard_map/ppermute | solution.py:33
  577.6 45.8 %collective-permute-start.77 = (bf16[1024,1024]{1,0:T(8,128)(2,1)}, bf16[1024,1024]{1,0:T(8,128)(2,1)}, u32[]{:S(2)}, u32[]{:S(2)}) collective-permute-start(bf16[1024,1024]{1,0:T(8,128)(2,1)} %shard_map.290), channel_id=1, source_target_pairs={{0,1},{1,0},{2,3},{3,2},{4,5},{5,4},{6,7},{7,6},{8,9},{9,8},{10,11... | collective-permute-start | bytes 6291464 | tf_op jit(solution)/shard_map/ppermute | solution.py:33
  578.1 31.6 %collective-permute-start.73 = (bf16[256,2048]{1,0:T(8,128)(2,1)}, bf16[256,2048]{1,0:T(8,128)(2,1)}, u32[]{:S(2)}, u32[]{:S(2)}) collective-permute-start(bf16[256,2048]{1,0:T(8,128)(2,1)} %get-tuple-element.835), channel_id=1, source_target_pairs={{0,8},{8,16},{16,24},{24,0},{1,9},{9,17},{17,25},{25,1},{2,10},{10... | collective-permute-start | bytes 3145736 | tf_op jit(solution)/shard_map/ppermute | solution.py:256
  623.4 32.3 %collective-permute-start.81 = (bf16[512,1024]{1,0:T(8,128)(2,1)}, bf16[512,1024]{1,0:T(8,128)(2,1)S(1)}, u32[]{:S(2)}, u32[]{:S(2)}) collective-permute-start(bf16[512,1024]{1,0:T(8,128)(2,1)} %get-tuple-element.866), channel_id=1, source_target_pairs={{0,4},{1,5},{2,6},{3,7},{4,0},{5,1},{6,2},{7,3},{8,12},{9,13},{10,... | collective-permute-start | bytes 3145736 | tf_op jit(solution)/shard_map/ppermute | solution.py:33
  624.0 31.7 %collective-permute-start.82 = (bf16[512,1024]{1,0:T(8,128)(2,1)}, bf16[512,1024]{1,0:T(8,128)(2,1)S(1)}, u32[]{:S(2)}, u32[]{:S(2)}) collective-permute-start(bf16[512,1024]{1,0:T(8,128)(2,1)} %get-tuple-element.868), channel_id=1, source_target_pairs={{0,2},{1,3},{2,0},{3,1},{4,6},{5,7},{6,4},{7,5},{8,10},{9,11},{10,... | collective-permute-start | bytes 3145736 | tf_op jit(solution)/shard_map/ppermute | solution.py:33
  625.5 27.3 %collective-permute-start.78 = (bf16[256,2048]{1,0:T(8,128)(2,1)}, bf16[256,2048]{1,0:T(8,128)(2,1)S(1)}, u32[]{:S(2)}, u32[]{:S(2)}) collective-permute-start(bf16[256,2048]{1,0:T(8,128)(2,1)} %shard_map.297), channel_id=1, source_target_pairs={{0,8},{8,16},{16,24},{24,0},{1,9},{9,17},{17,25},{25,1},{2,10},{10... | collective-permute-start | bytes 3145736 | tf_op jit(solution)/shard_map/ppermute | solution.py:256
  628.7 30.4 %collective-permute-start.79 = (bf16[512,512]{1,0:T(8,128)(2,1)}, bf16[512,512]{1,0:T(8,128)(2,1)S(1)}, u32[]{:S(2)}, u32[]{:S(2)}) collective-permute-start(bf16[512,512]{1,0:T(8,128)(2,1)} %get-tuple-element.862), channel_id=1, source_target_pairs={{0,4},{1,5},{2,6},{3,7},{4,0},{5,1},{6,2},{7,3},{8,12},{9,13},{10,... | collective-permute-start | bytes 1572872 | tf_op jit(solution)/shard_map/ppermute | solution.py:33
  629.6 29.9 %collective-permute-start.80 = (bf16[512,512]{1,0:T(8,128)(2,1)S(1)}, bf16[512,512]{1,0:T(8,128)(2,1)S(1)}, u32[]{:S(2)}, u32[]{:S(2)}) collective-permute-start(bf16[512,512]{1,0:T(8,128)(2,1)S(1)} %copy-done.178), channel_id=1, source_target_pairs={{0,2},{1,3},{2,0},{3,1},{4,6},{5,7},{6,4},{7,5},{8,10},{9,11},{10,... | collective-permute-start | bytes 1572872 | tf_op jit(solution)/shard_map/ppermute | solution.py:33
  (264 other events, 2729.5 us)
